TPU v7x, 1024 devices: a whole 4x4x32 slice. The times are simulated.
1024 devices in a mesh: pipe: 16 (over y_hi, x, core), expert: 32 (over z), dp: 2 (over y_lo).
Axes of the slice: x: 4, y: 4 (y_hi: 2, y_lo: 2; y = y_hi * 2 + y_lo), z: 32, core: 2. Of those that a mesh axis runs over, the one named last changes fastest.
Arguments:
- fwd_sent: bfloat16 [16, 512, 7168], P('pipe', 'dp', 'expert'), may hold values from -6 to 6
- fwd_route: int32 [16, 512, 1], P('pipe', 'dp'), may hold values from 0 to 1; in each aligned block of 256 rows (0 to 255, 256 to 511, ..., all dimensions but the last counted through in order) at most 144 rows name the same one
- fwd_weight: bfloat16 [16, 512, 1], P('pipe', 'dp'), may hold values from 0.099609375 to 1
- bwd_cot: bfloat16 [16, 512, 7168], P('pipe', 'dp', 'expert'), may hold values from -6 to 6
- bwd_route: int32 [16, 512, 1], P('pipe', 'dp'), may hold values from 0 to 1; in each aligned block of 256 rows (0 to 255, 256 to 511, ..., all dimensions but the last counted through in order) at most 144 rows name the same one
- bwd_weight: bfloat16 [16, 512, 1], P('pipe', 'dp'), may hold values from 0.099609375 to 1
- saved_gate: bfloat16 [16, 2, 144, 2048], P('pipe', 'dp', None, 'expert'), may hold values from -6 to 6
- saved_up: bfloat16 [16, 2, 144, 2048], P('pipe', 'dp', None, 'expert'), may hold values from -6 to 6
- gate_weight: bfloat16 [16, 2048, 7168], P('pipe', 'expert'), may hold values from -0.0625 to 0.0625
- up_weight: bfloat16 [16, 2048, 7168], P('pipe', 'expert'), may hold values from -0.0625 to 0.0625
- down_weight: bfloat16 [16, 2048, 7168], P('pipe', 'expert'), may hold values from -0.1875 to 0.1875
Outputs:
- fwd_out: bfloat16 [16, 512, 7168], P('pipe', 'dp', 'expert')
- bwd_grad: bfloat16 [16, 512, 7168], P('pipe', 'dp', 'expert')
- down_grad: float32 [16, 2048, 7168], P('pipe', ('expert', 'dp'))
Inputs may be any that keep to these rules, and one draw needn't show every extreme that they name: `fwd_route`: each row names 1 different experts. In each aligned block of 256 rows (the rows of one replica of a section) no expert is named by more than 144 rows, a bound that some block reaches. `bwd_route`: each row names 1 different experts. In each aligned block of 256 rows (the rows of one replica of a section) no expert is named by more than 144 rows, a bound that some block reaches.
All inputs are finite; a program needn't handle non-finite values.
Results may differ from a plain program's by a relative error of at most 0.0049.
Values may be sent and summed in bfloat16 or wider, within the bound.
A program may use at most 64 MiB of HBM per device.

v0:
```python
import jax
import jax.numpy as jnp
from jax import lax
from jax.sharding import PartitionSpec as P

EXPERTS = 2


def from_behind(value, axis, steps):
    count = lax.axis_size(axis)
    pairs = [(source, (source + steps) % count) for source in range(count)]
    return lax.ppermute(value, axis, pairs)


def layout(route, experts, capacity):
    tokens, topk = route.shape
    flat = route.reshape(tokens * topk)
    onehot = (flat[:, None] == jnp.arange(experts, dtype=jnp.int32)[None, :]).astype(jnp.int32)
    before = jnp.cumsum(onehot, axis=0) - onehot
    slot = jnp.sum(before * onehot, axis=1)
    target = flat * capacity + slot
    placed = (target[:, None] == jnp.arange(experts * capacity, dtype=jnp.int32)[None, :]).astype(
        jnp.float32
    )
    return placed.reshape(tokens, topk, experts * capacity)


def body(
    fwd_sent,
    fwd_route,
    fwd_weight,
    bwd_cot,
    bwd_route,
    bwd_weight,
    saved_gate,
    saved_up,
    gate_weight,
    up_weight,
    down_weight,
):
    arrived = from_behind(fwd_sent, "pipe", 1)[0]
    cotangent = from_behind(bwd_cot, "pipe", -1)[0]
    capacity = saved_gate.shape[2]
    owners = lax.axis_size("expert")
    split = owners // EXPERTS
    place_f = layout(fwd_route[0], EXPERTS, capacity)
    place_b = layout(bwd_route[0], EXPERTS, capacity)
    select_f = jnp.sum(place_f, axis=1).astype(jnp.bfloat16)
    mix_f = jnp.sum(fwd_weight[0].astype(jnp.float32)[:, :, None] * place_f, axis=1).astype(
        jnp.bfloat16
    )
    scale_b = jnp.sum(bwd_weight[0].astype(jnp.float32)[:, :, None] * place_b, axis=1).astype(
        jnp.bfloat16
    )
    ones_b = jnp.sum(place_b, axis=1).astype(jnp.bfloat16)
    by_rows = (((0,), (0,)), ((), ()))
    by_units = (((1,), (1,)), ((), ()))
    send_f = lax.dot_general(select_f, arrived, by_rows, preferred_element_type=jnp.float32).astype(
        jnp.bfloat16
    )
    send_b = lax.dot_general(
        scale_b, cotangent, by_rows, preferred_element_type=jnp.float32
    ).astype(jnp.bfloat16)
    local_width = send_f.shape[1]
    spread_f = jnp.broadcast_to(
        send_f.reshape(EXPERTS, 1, capacity, local_width), (EXPERTS, split, capacity, local_width)
    ).reshape(owners, capacity, local_width)
    spread_b = jnp.broadcast_to(
        send_b.reshape(EXPERTS, 1, capacity, local_width), (EXPERTS, split, capacity, local_width)
    ).reshape(owners, capacity, local_width)
    recv_f, recv_b = (
        lax.all_to_all(spread_f, "expert", split_axis=0, concat_axis=2, tiled=True),
        lax.all_to_all(spread_b, "expert", split_axis=0, concat_axis=2, tiled=True),
    )
    rows_f = recv_f[0]
    rows_b = recv_b[0]
    w_gate = gate_weight[0]
    w_up = up_weight[0]
    w_down = down_weight[0]
    gate = lax.dot_general(rows_f, w_gate, by_units, preferred_element_type=jnp.float32)
    upper = lax.dot_general(rows_f, w_up, by_units, preferred_element_type=jnp.float32)
    hidden = (gate * jax.nn.sigmoid(gate) * upper).astype(jnp.bfloat16)
    part_f = jnp.dot(hidden, w_down, preferred_element_type=jnp.float32).astype(jnp.bfloat16)
    gate_b = saved_gate[0, 0].astype(jnp.float32)
    upper_b = saved_up[0, 0].astype(jnp.float32)
    sig = jax.nn.sigmoid(gate_b)
    hidden_b = (gate_b * sig * upper_b).astype(jnp.bfloat16)
    d_hidden = lax.dot_general(rows_b, w_down, by_units, preferred_element_type=jnp.float32)
    d_gate = (d_hidden * upper_b * sig * (1.0 + gate_b * (1.0 - sig))).astype(jnp.bfloat16)
    d_up = (d_hidden * gate_b * sig).astype(jnp.bfloat16)
    part_b = jnp.dot(d_gate, w_gate, preferred_element_type=jnp.float32)
    part_b = (part_b + jnp.dot(d_up, w_up, preferred_element_type=jnp.float32)).astype(jnp.bfloat16)
    back_f, back_b = (
        lax.all_to_all(
            part_f.reshape(1, capacity, owners, -1),
            "expert",
            split_axis=2,
            concat_axis=0,
            tiled=True,
        ),
        lax.all_to_all(
            part_b.reshape(1, capacity, owners, -1),
            "expert",
            split_axis=2,
            concat_axis=0,
            tiled=True,
        ),
    )
    expert_out = (
        jnp.sum(back_f.reshape(EXPERTS, split, capacity, -1).astype(jnp.float32), axis=1)
        .astype(jnp.bfloat16)
        .reshape(EXPERTS * capacity, -1)
    )
    expert_grad = (
        jnp.sum(back_b.reshape(EXPERTS, split, capacity, -1).astype(jnp.float32), axis=1)
        .astype(jnp.bfloat16)
        .reshape(EXPERTS * capacity, -1)
    )
    forward = (
        arrived.astype(jnp.float32) + jnp.dot(mix_f, expert_out, preferred_element_type=jnp.float32)
    ).astype(jnp.bfloat16)
    backward = (
        cotangent.astype(jnp.float32)
        + jnp.dot(ones_b, expert_grad, preferred_element_type=jnp.float32)
    ).astype(jnp.bfloat16)
    share = lax.psum_scatter(
        lax.dot_general(hidden_b, rows_b, by_rows, preferred_element_type=jnp.float32),
        "dp",
        scatter_dimension=0,
        tiled=True,
    )
    return (forward[None], backward[None], share[None])


def solution(mesh):
    in_specs = (
        P("pipe", "dp", "expert"),
        P("pipe", "dp", None),
        P("pipe", "dp", None),
        P("pipe", "dp", "expert"),
        P("pipe", "dp", None),
        P("pipe", "dp", None),
        P("pipe", "dp", None, "expert"),
        P("pipe", "dp", None, "expert"),
        P("pipe", "expert", None),
        P("pipe", "expert", None),
        P("pipe", "expert", None),
    )
    out_specs = (
        P("pipe", "dp", "expert"),
        P("pipe", "dp", "expert"),
        P("pipe", ("expert", "dp"), None),
    )
    return jax.shard_map(body, mesh=mesh, in_specs=in_specs, out_specs=out_specs, check_vma=False)
```

profile of v0, /device:TPU:24, one launch (start us, length us, event | category | flops | bytes accessed | tf_op | source)
XLA Modules:
  0.0 950.8 jit_solution(6003289251779076522)
XLA Ops:
  7.2 2.1 collective-permute-start
  12.4 4.9 collective-permute-done
  17.5 1.6 broadcast_in_dim.15
  19.0 28.9 %all-to-all-start = ((bf16[32,144,224]{2,1,0:T(8,128)(2,1)}), bf16[32,144,224]{2,1,0:T(8,128)(2,1)S(1)}, u32[]{:S(2)}, u32[]{:S(2)}) async-start(bf16[32,144,224]{2,1,0:T(8,128)(2,1)} %bitcast.168), calls=%async_computation | async-start | bytes 4718592 | tf_op jit(solution)/shard_map/all_to_all | solution.py:72
  47.9 2.1 collective-permute-start.1
  51.2 1.2 collective-permute-done.1
  52.4 1.1 convolution_convert_fusion.1
  53.5 212.1 %all-to-all-done = bf16[32,144,224]{2,1,0:T(8,128)(2,1)S(1)} async-done(((bf16[32,144,224]{2,1,0:T(8,128)(2,1)}), bf16[32,144,224]{2,1,0:T(8,128)(2,1)S(1)}, u32[]{:S(2)}, u32[]{:S(2)}) %all-to-all-start) | async-done | bytes 2064416 | tf_op jit(solution)/shard_map/all_to_all | solution.py:72
  265.6 1.6 broadcast_in_dim.35
  267.2 4.8 all-to-all-start.2
  272.0 2.2 copy.22
  274.2 4.7 squeeze.26
  278.9 2.0 fusion.10
  280.9 4.9 convolution_convert_fusion
  285.9 4.7 reshape.327
  290.6 2.7 copy.23
  293.3 197.1 %all-to-all-done.2 = bf16[32,144,224]{2,1,0:T(8,128)(2,1)} async-done(((bf16[32,144,224]{2,1,0:T(8,128)(2,1)}), bf16[32,144,224]{2,1,0:T(8,128)(2,1)}, u32[]{:S(2)}, u32[]{:S(2)}) %all-to-all-start.2) | async-done | bytes 2064416 | tf_op jit(solution)/shard_map/all_to_all | solution.py:73
  490.4 5.0 all-to-all-start.1
  495.4 3.9 copy.26
  499.3 4.7 squeeze.31
  504.0 2.1 fusion.2
  506.8 2.1 fusion
  509.0 5.7 reshape.332
  514.7 4.4 copy.27
  519.1 196.9 %all-to-all-done.1 = bf16[1,144,32,224]{3,1,0,2:T(8,128)(2,1)} async-done(((bf16[1,144,32,224]{3,1,0,2:T(8,128)(2,1)}), bf16[1,144,32,224]{3,1,0,2:T(8,128)(2,1)}, u32[]{:S(2)}, u32[]{:S(2)}) %all-to-all-start.1) | async-done | bytes 2064416 | tf_op jit(solution)/shard_map/all_to_all | solution.py:94
  716.0 4.8 all-to-all-start.3
  720.9 1.8 fusion.66
  722.7 2.1 reduce_sum.48
  724.7 214.5 %all-to-all-done.3 = bf16[1,144,32,224]{3,1,0,2:T(8,128)(2,1)} async-done(((bf16[1,144,32,224]{3,1,0,2:T(8,128)(2,1)}), bf16[1,144,32,224]{3,1,0,2:T(8,128)(2,1)}, u32[]{:S(2)}, u32[]{:S(2)}) %all-to-all-start.3) | async-done | bytes 2064416 | tf_op jit(solution)/shard_map/all_to_all | solution.py:101
  939.2 2.1 reduce_sum.50
  941.3 1.8 fusion.27
  943.1 0.9 fusion.17
  (37 shorter events, 5.3 us)
Async XLA Ops:
  7.2 273.7 %copy-start = (bf16[1,64,7168]{2,1,0:T(8,128)(2,1)S(1)}, bf16[1,64,7168]{2,1,0:T(8,128)(2,1)}, u32[]{:S(2)}) copy-start(bf16[1,64,7168]{2,1,0:T(8,128)(2,1)} %param.20) | copy-start | bytes 2752516
  7.2 10.1 %collective-permute-start = (bf16[1,256,224]{1,2,0:T(8,128)(2,1)}, bf16[1,256,224]{1,2,0:T(8,128)(2,1)S(1)}, u32[]{:S(2)}, u32[]{:S(2)}) collective-permute-start(bf16[1,256,224]{1,2,0:T(8,128)(2,1)} %param.11), channel_id=1, source_target_pairs={{0,64},{64,128},{128,192},{192,256},{256,320},{320,384},{384,448},... | collective-permute-start | bytes 344072 | tf_op jit(solution)/shard_map/ppermute | solution.py:12
  19.0 28.9 %copy-start.7 = (bf16[1,256,224]{1,2,0:T(8,128)(2,1)S(1)}, bf16[1,256,224]{1,2,0:T(8,128)(2,1)}, u32[]{:S(2)}) copy-start(bf16[1,256,224]{1,2,0:T(8,128)(2,1)} %param.14) | copy-start | bytes 344068
  19.0 31.0 %copy-start.5 = (bf16[1,256,1]{1,2,0:T(2,128)(2,1)S(1)}, bf16[1,256,1]{1,2,0:T(2,128)(2,1)}, u32[]{:S(2)}) copy-start(bf16[1,256,1]{1,2,0:T(2,128)(2,1)} %param.16) | copy-start | bytes 1540
  19.0 31.0 %copy-start.4 = (s32[1,256,1]{1,2,0:T(1,128)S(1)}, s32[1,256,1]{1,2,0:T(1,128)}, u32[]{:S(2)}) copy-start(s32[1,256,1]{1,2,0:T(1,128)} %param.15) | copy-start | bytes 3076
  19.0 246.6 %all-to-all-start = ((bf16[32,144,224]{2,1,0:T(8,128)(2,1)}), bf16[32,144,224]{2,1,0:T(8,128)(2,1)S(1)}, u32[]{:S(2)}, u32[]{:S(2)}) async-start(bf16[32,144,224]{2,1,0:T(8,128)(2,1)} %bitcast.168), calls=%async_computation | async-start | bytes 4718592 | tf_op jit(solution)/shard_map/all_to_all | solution.py:72
  47.9 4.5 collective-permute-start.1
  267.2 223.2 %all-to-all-start.2 = ((bf16[32,144,224]{2,1,0:T(8,128)(2,1)}), bf16[32,144,224]{2,1,0:T(8,128)(2,1)}, u32[]{:S(2)}, u32[]{:S(2)}) async-start(bf16[32,144,224]{2,1,0:T(8,128)(2,1)} %bitcast.169), calls=%async_computation.2 | async-start | bytes 4718592 | tf_op jit(solution)/shard_map/all_to_all | solution.py:73
  490.4 225.6 %all-to-all-start.1 = ((bf16[1,144,32,224]{3,1,0,2:T(8,128)(2,1)}), bf16[1,144,32,224]{3,1,0,2:T(8,128)(2,1)}, u32[]{:S(2)}, u32[]{:S(2)}) async-start(bf16[1,144,32,224]{3,1,0,2:T(8,128)(2,1)} %copy.23), calls=%async_computation.1 | async-start | bytes 4718592 | tf_op jit(solution)/shard_map/all_to_all | solution.py:94
  504.0 2.1 copy-start.1
  504.0 2.1 copy-start.2
  504.0 2.1 copy-start.3
  716.0 223.2 %all-to-all-start.3 = ((bf16[1,144,32,224]{3,1,0,2:T(8,128)(2,1)}), bf16[1,144,32,224]{3,1,0,2:T(8,128)(2,1)}, u32[]{:S(2)}, u32[]{:S(2)}) async-start(bf16[1,144,32,224]{3,1,0,2:T(8,128)(2,1)} %copy.27), calls=%async_computation.3 | async-start | bytes 4718592 | tf_op jit(solution)/shard_map/all_to_all | solution.py:101
  720.8 1.8 copy-start.6
  720.8 223.2 %reduce-scatter.2.cloned.1.call-start = ((), (), s32[]{:S(2)}) async-start(), calls=%async_computation.5 | async-start | bytes 2752512 | tf_op jit(solution)/shard_map/reduce_scatter | solution.py:126
Sparse Core Ops, SparseCore 0:
  725.6 49.4 reduce-scatter.1
where the time goes:
time: 952 us; the launch traced here: 951 us
  waiting for transfers between devices  827 us (87%)
  starting transfers between devices  47.7 us (5%)
  local copies, waits for them, and re-layouts  36.6 us (4%)
  matrix products  17.7 us (2%)
  between operations  14.3 us (2%)
    all_to_all x1, waiting for transfers between devices, body(): lax.all_to_all(part_b.reshape(1, capacity, owners, -1), 'expert', split_a...  214 us
    all_to_all x1, waiting for transfers between devices, body(): lax.all_to_all(spread_f, 'expert', split_axis=0, concat_axis=2, tiled=True)  212 us
    all_to_all x1, waiting for transfers between devices, body(): lax.all_to_all(spread_b, 'expert', split_axis=0, concat_axis=2, tiled=True)  197 us
    all_to_all x1, waiting for transfers between devices, body(): lax.all_to_all(part_f.reshape(1, capacity, owners, -1), 'expert', split_a...  197 us
    all_to_all x1, starting transfers between devices, body(): lax.all_to_all(spread_f, 'expert', split_axis=0, concat_axis=2, tiled=True)  28.9 us
  transfers between devices with their start and end apart: 7, of which 6 were waited for; matrix products, arithmetic and copies ran while one was open for 6% of the time, Pallas kernels for 0%

commit v1 on v0

v1 whole, which is shorter than its diff:
```python
import functools

import jax
import jax.numpy as jnp
from jax import lax
from jax.experimental import pallas as pl
from jax.experimental.pallas import tpu as pltpu
from jax.sharding import PartitionSpec as P

EXPERTS = 2
LANES = 128
MESH = pl.DeviceIdType.MESH
BY_UNITS = (((1,), (1,)), ((), ()))
F32 = jnp.float32
BF16 = jnp.bfloat16


def dot(a, b):
    return jnp.dot(a, b, preferred_element_type=F32)


def dot_t(a, b):
    return lax.dot_general(a, b, BY_UNITS, preferred_element_type=F32)


def pack(main, tail, rest):
    quarter = tail.shape[0] // 4
    spare = LANES - rest
    lane = lax.broadcasted_iota(jnp.int32, (quarter, LANES), 1)
    last = tail[3 * quarter :]
    parts = [main]
    for k in range(3):
        moved = pltpu.roll(last, rest - spare * k, axis=1)
        parts.append(jnp.where(lane < rest, tail[k * quarter : (k + 1) * quarter], moved))
    return jnp.concatenate(parts, axis=0)


def unpack(packed, rows, rest):
    quarter = rows // 4
    spare = LANES - rest
    lane = lax.broadcasted_iota(jnp.int32, (quarter, LANES), 1)
    pieces = [packed[rows + k * quarter : rows + (k + 1) * quarter] for k in range(3)]
    last = pltpu.roll(pieces[2].astype(F32), LANES - rest + 2 * spare, axis=1)
    for k in (1, 0):
        moved = pltpu.roll(pieces[k].astype(F32), LANES - rest + k * spare, axis=1)
        last = jnp.where(lane < (k + 1) * spare, moved, last)
    tail = jnp.concatenate(pieces + [last.astype(packed.dtype)], axis=0)
    return packed[:rows], tail


def kernel(
    ring,
    sections,
    x_ref,
    froute_ref,
    fweight_ref,
    c_ref,
    broute_ref,
    bweight_ref,
    sgate_ref,
    sup_ref,
    wg_ref,
    wu_ref,
    wd_ref,
    fout_ref,
    bout_ref,
    dgrad_ref,
    xs,
    cs,
    craw,
    gath_f,
    gath_b,
    red_f,
    red_b,
    wgu,
    wdn,
    acc_f,
    acc_b,
    coef_g,
    coef_u,
    hbt,
    hid,
    dgu,
    dg,
    dg_in,
    pipe_send,
    pipe_recv,
    gs_f,
    gr_f,
    gs_b,
    gr_b,
    rs_f,
    rr_f,
    rs_b,
    rr_b,
    dp_send,
    dp_recv,
):
    rows, width = x_ref.shape
    units = wg_ref.shape[0]
    capacity = sgate_ref.shape[0]
    rest = width - LANES
    half = ring // 2
    quarter = rows // 4
    dense = rows + 3 * quarter
    me = lax.axis_index("expert")
    section = lax.axis_index("pipe")
    replica = lax.axis_index("dp")
    right, left = lax.rem(me + 1, ring), lax.rem(me + ring - 1, ring)
    ahead, behind = lax.rem(section + 1, sections), lax.rem(section + sections - 1, sections)
    peer = 1 - replica
    expert = me // (ring // EXPERTS)

    barrier = pltpu.get_barrier_semaphore()
    for axis, other in (
        ("expert", right),
        ("expert", left),
        ("pipe", ahead),
        ("pipe", behind),
        ("dp", peer),
    ):
        pl.semaphore_signal(barrier, inc=1, device_id={axis: other}, device_id_type=MESH)

    def to_dense(ref):
        value = ref[...].astype(F32)
        tail = jnp.concatenate([value[:, LANES:], jnp.zeros((rows, LANES - rest), F32)], axis=1)
        return pack(value[:, :LANES], tail, rest).astype(BF16)

    xs[...] = to_dense(x_ref)
    cs[...] = to_dense(c_ref)
    pl.semaphore_wait(barrier, 5)

    def shift(k):
        return pltpu.make_async_remote_copy(
            src_ref=(xs, cs)[k],
            dst_ref=(gath_f.at[me], craw)[k],
            send_sem=pipe_send.at[k],
            recv_sem=pipe_recv.at[k],
            device_id={"pipe": (ahead, behind)[k]},
            device_id_type=MESH,
        )

    shift(0).start()
    shift(1).start()

    gap = jnp.zeros((units, 2 * LANES - width), BF16)
    for z in range(ring):
        columns = slice(z * width, (z + 1) * width)
        wgu[z, :units, :] = jnp.concatenate([wg_ref[:, columns], gap], axis=1)
        wgu[z, units:, :] = jnp.concatenate([wu_ref[:, columns], gap], axis=1)
        wdn[z] = jnp.concatenate([wd_ref[:, columns], gap], axis=1)

    mine = broute_ref[...] == expert
    before = (
        lax.broadcasted_iota(jnp.int32, (rows, rows), 0)
        > lax.broadcasted_iota(jnp.int32, (rows, rows), 1)
    ).astype(F32).astype(BF16)
    named = jnp.broadcast_to(mine.astype(F32), (rows, capacity))
    slot = dot(before, named.astype(BF16))
    column = lax.broadcasted_iota(jnp.int32, (rows, capacity), 1).astype(F32)
    place = jnp.where(slot == column, named, 0.0).astype(BF16)
    gate_b = dot(place, sgate_ref[...])
    upper_b = dot(place, sup_ref[...])
    sig = jax.nn.sigmoid(gate_b)
    coef_g[...] = upper_b * sig * (1.0 + gate_b * (1.0 - sig))
    coef_u[...] = gate_b * sig
    hbt[...] = jnp.transpose(gate_b * sig * upper_b).astype(BF16)

    def ring_copy(buf, slot_out, slot_in, send, recv, way, k):
        return pltpu.make_async_remote_copy(
            src_ref=buf.at[slot_out],
            dst_ref=buf.at[slot_in],
            send_sem=send.at[way, k],
            recv_sem=recv.at[way, k],
            device_id={"expert": (right, left)[way]},
            device_id_type=MESH,
        )

    def gather(stream, way, k):
        buf, send, recv = ((gath_f, gs_f, gr_f), (gath_b, gs_b, gr_b))[stream]
        shard = lax.rem(me + ring - k, ring) if way == 0 else lax.rem(me + k, ring)
        return ring_copy(buf, shard, shard, send, recv, way, k)

    def arrived(stream, way, k):
        buf, send, recv = ((gath_f, gs_f, gr_f), (gath_b, gs_b, gr_b))[stream]
        shard = lax.rem(me + ring - 1 - k, ring) if way == 0 else lax.rem(me + 1 + k, ring)
        ring_copy(buf, shard, shard, send, recv, way, k).wait_recv()
        return shard

    def use_f(shard):
        main, tail = unpack(gath_f[shard], rows, rest)
        acc_f[...] += dot_t(jnp.concatenate([main, tail], axis=1), wgu[shard])

    def use_b(shard):
        main, tail = unpack(gath_b[shard], rows, rest)
        acc_b[...] += dot_t(jnp.concatenate([main, tail], axis=1), wdn[shard])

    acc_f[...] = jnp.zeros_like(acc_f)
    acc_b[...] = jnp.zeros_like(acc_b)

    shift(0).wait_recv()
    gather(0, 0, 0).start()
    gather(0, 1, 0).start()
    shift(1).wait_recv()
    bweight = bweight_ref[...].astype(F32)
    lane = lax.broadcasted_iota(jnp.int32, (quarter, LANES), 1)
    scales = [jnp.broadcast_to(bweight, (rows, LANES))]
    for k in range(3):
        scales.append(
            jnp.where(lane < rest, bweight[k * quarter : (k + 1) * quarter], bweight[3 * quarter :])
        )
    gath_b[me] = (craw[...].astype(F32) * jnp.concatenate(scales, axis=0)).astype(BF16)
    gather(1, 0, 0).start()
    gather(1, 1, 0).start()
    use_f(me)
    use_b(me)

    def gather_both(k, carry):
        for stream, use in ((0, use_f), (1, use_b)):
            one = arrived(stream, 0, k)
            gather(stream, 0, k + 1).start()
            two = arrived(stream, 1, k)

            @pl.when(k < half - 2)
            def _():
                gather(stream, 1, k + 1).start()

            use(one)
            use(two)
        return carry

    lax.fori_loop(0, half - 1, gather_both, 0)
    last_f = arrived(0, 0, half - 1)
    use_f(last_f)
    gate = acc_f[:, :units]
    upper = acc_f[:, units:]
    hid[...] = jnp.where(
        froute_ref[...] == expert, gate * jax.nn.sigmoid(gate) * upper, 0.0
    ).astype(BF16)

    def part_f(shard):
        full = dot(hid[...], wdn[shard])
        return pack(full[:, :LANES], full[:, LANES:], rest)

    def part_b(shard):
        full = dot(dgu[...], wgu[shard])
        return pack(full[:, :LANES], full[:, LANES:], rest)

    def reduce(stream, way, k):
        buf, send, recv = ((red_f, rs_f, rr_f), (red_b, rs_b, rr_b))[stream]
        return pltpu.make_async_remote_copy(
            src_ref=buf.at[way, k],
            dst_ref=buf.at[way, k + 1],
            send_sem=send.at[way, k],
            recv_sem=recv.at[way, k],
            device_id={"expert": (right, left)[way]},
            device_id_type=MESH,
        )

    def target(way, k):
        return lax.rem(me + half - k + ring, ring) if way == 0 else lax.rem(me + ring - half + 1 + k, ring)

    for way in range(2):
        red_f[way, 0] = part_f(target(way, 0)).astype(BF16)
        reduce(0, way, 0).start()

    last_b = arrived(1, 0, half - 1)
    use_b(last_b)
    d_hidden = acc_b[...]
    dgu[:, :units] = (d_hidden * coef_g[...]).astype(BF16)
    dgu[:, units:] = (d_hidden * coef_u[...]).astype(BF16)
    for way in range(2):
        red_b[way, 0] = part_b(target(way, 0)).astype(BF16)
        reduce(1, way, 0).start()

    def down_piece(g):
        pieces = []
        for z in range(4):
            main, tail = unpack(gath_b[4 * g + z], rows, rest)
            full = dot(hbt[...], jnp.concatenate([main, tail], axis=1))
            pieces.append(full[:, :width])
        start = pl.multiple_of(g * 4 * width, LANES)
        dg[:, pl.ds(start, 4 * width)] = jnp.concatenate(pieces, axis=1)

    def reduce_step(k):
        for stream, part in ((0, part_f), (1, part_b)):
            buf = (red_f, red_b)[stream]
            reduce(stream, 0, k - 1).wait_recv()
            buf[0, k] = (buf[0, k].astype(F32) + part(target(0, k))).astype(BF16)
            reduce(stream, 0, k).start()

            @pl.when(k < half - 1)
            def _():
                reduce(stream, 1, k - 1).wait_recv()
                buf[1, k] = (buf[1, k].astype(F32) + part(target(1, k))).astype(BF16)
                reduce(stream, 1, k).start()

    groups = ring // 4

    def early(k, carry):
        reduce_step(k)
        down_piece(k - 1)
        return carry

    def late(k, carry):
        reduce_step(k)
        return carry

    def give():
        return pltpu.make_async_remote_copy(
            src_ref=dg.at[pl.ds(pl.multiple_of(peer * (units // 2), 8), units // 2)],
            dst_ref=dg_in,
            send_sem=dp_send,
            recv_sem=dp_recv,
            device_id={"dp": peer},
            device_id_type=MESH,
        )

    lax.fori_loop(1, groups + 1, early, 0)
    give().start()
    lax.fori_loop(groups + 1, half, late, 0)

    for stream, part in ((0, part_f), (1, part_b)):
        buf = (red_f, red_b)[stream]
        total = part(me)
        reduce(stream, 1, half - 2).wait_recv()
        total = total + buf[1, half - 1].astype(F32)
        reduce(stream, 0, half - 1).wait_recv()
        total = total + buf[0, half].astype(F32)
        main, tail = unpack(total, rows, rest)
        summed = jnp.concatenate([main, tail[:, :rest]], axis=1).astype(BF16).astype(F32)
        own_main, own_tail = unpack((gath_f[me], craw[...])[stream], rows, rest)
        own = jnp.concatenate([own_main, own_tail], axis=1)[:, :width].astype(F32)
        if stream == 0:
            fout_ref[...] = (own + fweight_ref[...].astype(F32) * summed).astype(BF16)
        else:
            bout_ref[...] = (own + summed).astype(BF16)

    give().wait_recv()
    mine_rows = pl.ds(pl.multiple_of(replica * (units // 2), 8), units // 2)
    dgrad_ref[...] = dg[mine_rows, :] + dg_in[...]

    shift(0).wait_send()
    shift(1).wait_send()
    give().wait_send()
    for stream in range(2):
        for way, count in ((0, half), (1, half - 1)):

            def drain(k, carry):
                gather(stream, way, k).wait_send()
                reduce(stream, way, k).wait_send()
                return carry

            lax.fori_loop(0, count, drain, 0)


def solution(mesh):
    ring = mesh.shape["expert"]
    sections = mesh.shape["pipe"]
    half = ring // 2

    def body(
        fwd_sent,
        fwd_route,
        fwd_weight,
        bwd_cot,
        bwd_route,
        bwd_weight,
        saved_gate,
        saved_up,
        gate_weight,
        up_weight,
        down_weight,
    ):
        rows, width = fwd_sent.shape[1:]
        units, model = gate_weight.shape[1:]
        dense = rows + 3 * (rows // 4)
        dma = pltpu.SemaphoreType.DMA
        vmem = pl.BlockSpec(memory_space=pltpu.VMEM)
        outs = pl.pallas_call(
            functools.partial(kernel, ring, sections),
            out_shape=(
                jax.ShapeDtypeStruct((rows, width), BF16),
                jax.ShapeDtypeStruct((rows, width), BF16),
                jax.ShapeDtypeStruct((units // 2, model), F32),
            ),
            in_specs=[vmem] * 11,
            out_specs=(vmem,) * 3,
            scratch_shapes=[
                pltpu.VMEM((dense, LANES), BF16),
                pltpu.VMEM((dense, LANES), BF16),
                pltpu.VMEM((dense, LANES), BF16),
                pltpu.VMEM((ring, dense, LANES), BF16),
                pltpu.VMEM((ring, dense, LANES), BF16),
                pltpu.VMEM((2, half + 1, dense, LANES), BF16),
                pltpu.VMEM((2, half + 1, dense, LANES), BF16),
                pltpu.VMEM((ring, 2 * units, 2 * LANES), BF16),
                pltpu.VMEM((ring, units, 2 * LANES), BF16),
                pltpu.VMEM((rows, 2 * units), F32),
                pltpu.VMEM((rows, units), F32),
                pltpu.VMEM((rows, units), F32),
                pltpu.VMEM((rows, units), F32),
                pltpu.VMEM((units, rows), BF16),
                pltpu.VMEM((rows, units), BF16),
                pltpu.VMEM((rows, 2 * units), BF16),
                pltpu.VMEM((units, model), F32),
                pltpu.VMEM((units // 2, model), F32),
                dma((2,)),
                dma((2,)),
            ]
            + [dma((2, half))] * 8
            + [dma, dma],
            compiler_params=pltpu.CompilerParams(
                collective_id=0, has_side_effects=True, vmem_limit_bytes=56 * 1024 * 1024
            ),
        )(
            fwd_sent[0],
            fwd_route[0],
            fwd_weight[0],
            bwd_cot[0],
            bwd_route[0],
            bwd_weight[0],
            saved_gate[0, 0],
            saved_up[0, 0],
            gate_weight[0],
            up_weight[0],
            down_weight[0],
        )
        return tuple(out[None] for out in outs)

    in_specs = (
        P("pipe", "dp", "expert"),
        P("pipe", "dp", None),
        P("pipe", "dp", None),
        P("pipe", "dp", "expert"),
        P("pipe", "dp", None),
        P("pipe", "dp", None),
        P("pipe", "dp", None, "expert"),
        P("pipe", "dp", None, "expert"),
        P("pipe", "expert", None),
        P("pipe", "expert", None),
        P("pipe", "expert", None),
    )
    out_specs = (
        P("pipe", "dp", "expert"),
        P("pipe", "dp", "expert"),
        P("pipe", ("expert", "dp"), None),
    )
    return jax.shard_map(body, mesh=mesh, in_specs=in_specs, out_specs=out_specs, check_vma=False)
```

time: 952 us -> 207 us (0.22)
  waiting for transfers between devices: 827 us -> 0 us
  Pallas kernels: 0 us -> 193 us
  starting transfers between devices: 47.7 us -> 0 us
  local copies, waits for them, and re-layouts: 36.6 us -> 12.2 us
  matrix products: 17.7 us -> 0 us
  between operations: 14.3 us -> 0.67 us
    all_to_all x4 -> x0, waiting for transfers between devices: 821 us -> none  [the longest x1 214 us: body(): lax.all_to_all(part_b.reshape(1, capacity, owners, -1), 'expert', split_a...]
    pallas_call x0 -> x1, Pallas kernels: none -> 193 us  [body(): pl.pallas_call(functools.partial(kernel, ring, sections), out_shape=(jax....]
    all_to_all x4 -> x0, starting transfers between devices: 43.4 us -> none  [the longest x1 28.9 us: body(): lax.all_to_all(spread_f, 'expert', split_axis=0, concat_axis=2, tiled=True)]
    dot_general x10 -> x0, matrix products: 17.7 us -> none  [the longest x1 4.95 us: body(): jnp.dot(hidden, w_down, preferred_element_type=jnp.float32)]
    reshape x4 -> x0, local copies, waits for them, and re-layouts: 17.6 us -> none  [the longest x2 10.2 us: body(): part_b.reshape(1, capacity, owners, -1)]
  transfers between devices with their start and end apart: 7 -> 0, of which waited for: 6 -> 0; matrix products, arithmetic and copies ran while one was open for 6% -> 0% of each run, Pallas kernels for 0% -> 0%
where the time goes in v1:
time: 207 us; the launch traced here: 206 us
  Pallas kernels  193 us (93%)
  local copies, waits for them, and re-layouts  12.2 us (6%)
    pallas_call x1, Pallas kernels, body(): pl.pallas_call(functools.partial(kernel, ring, sections), out_shape=(jax....  193 us
    unnamed x23, local copies, waits for them, and re-layouts  9.13 us

profile of v1, /device:TPU:24, one launch (start us, length us, event | category | flops | bytes accessed | tf_op | source)
XLA Modules:
  0.0 205.7 jit_solution(12865375264777421410)
XLA Ops:
  0.6 0.0 copy-start.3
  0.6 0.0 copy-start.4
  0.7 1.5 copy.22
  2.1 0.0 copy-start.1
  2.1 0.0 copy-done.3
  2.1 0.7 copy.23
  2.9 0.0 copy-done.4
  2.9 0.0 copy-start.5
  2.9 0.8 copy.25.fweight_ref
  3.6 0.0 copy-done.5
  3.6 0.8 copy.27.bweight_ref
  4.4 0.0 copy-done.1
  4.4 0.0 copy-start.6
  4.4 0.8 copy.20
  5.1 0.0 copy-start.2
  5.1 0.0 copy-done.6
  5.2 0.8 copy.24.froute_ref
  5.9 0.1 copy-done.2
  6.0 0.8 copy.21
  6.8 0.0 copy-start.7
  6.8 0.7 copy-done.7
  7.5 0.8 copy.26.broute_ref
  8.3 192.8 %shard_map.130 = (bf16[256,224]{1,0:T(8,128)(2,1)}, bf16[256,224]{1,0:T(8,128)(2,1)}, f32[32,7168]{1,0:T(8,128)}) custom-call(bf16[256,224]{1,0:T(8,128)(2,1)} %bitcast.18, s32[256,1]{1,0:T(8,128)} %copy.24.froute_ref, bf16[256,1]{1,0:T(8,128)(2,1)} %copy.25.fweight_ref, bf16[256,224]{1,0:T(8,128)(2,1)} %bitcast.19, s32[256,1]{1,0:T(8,128)} %copy.26.broute_ref, ...), custom_call_target="tpu_custom_call" | custom-call | tf_op jit(solution)/shard_map/pallas_call | solution.py:380
  201.1 0.0 copy-start
  201.1 1.7 copy.28
  202.8 0.0 copy-done
  202.8 0.8 copy.29
  203.6 2.2 %copy.31 = f32[1,32,7168]{2,1,0:T(8,128)} copy(f32[1,32,7168]{2,1,0:T(8,128)} %bitcast.14) | data formatting | bytes 1835008
Async XLA Ops:
  0.6 1.5 copy-start.3
  0.6 2.2 %copy-start.4 = (bf16[1,256,1]{1,2,0:T(2,128)(2,1)S(1)}, bf16[1,256,1]{1,2,0:T(2,128)(2,1)}, u32[]{:S(2)}) copy-start(bf16[1,256,1]{1,2,0:T(2,128)(2,1)} %param.13) | copy-start | bytes 1540
  2.1 2.2 %copy-start.1 = (bf16[1,256,224]{1,2,0:T(8,128)(2,1)S(1)}, bf16[1,256,224]{1,2,0:T(8,128)(2,1)}, u32[]{:S(2)}) copy-start(bf16[1,256,224]{1,2,0:T(8,128)(2,1)} %param.11) | copy-start | bytes 344068
  2.9 0.8 copy-start.5
  4.4 0.8 copy-start.6
  5.1 0.9 copy-start.2
  6.8 0.7 copy-start.7
  201.1 1.7 copy-start

commit v2 on v1

v2 whole, which is shorter than its diff:
```python
import functools

import jax
import jax.numpy as jnp
from jax import lax
from jax.experimental import pallas as pl
from jax.experimental.pallas import tpu as pltpu
from jax.sharding import PartitionSpec as P

EXPERTS = 2
LANES = 128
GROUP = 4
MESH = pl.DeviceIdType.MESH
BY_UNITS = (((1,), (1,)), ((), ()))
F32 = jnp.float32
BF16 = jnp.bfloat16


def dot(a, b):
    return jnp.dot(a, b, preferred_element_type=F32)


def dot_t(a, b):
    return lax.dot_general(a, b, BY_UNITS, preferred_element_type=F32)


def kernel(
    ring,
    sections,
    x_ref,
    froute_ref,
    fweight_ref,
    c_ref,
    broute_ref,
    bweight_ref,
    sgate_ref,
    sup_ref,
    wg_ref,
    wu_ref,
    wd_ref,
    fout_ref,
    bout_ref,
    dgrad_ref,
    craw,
    gath_f,
    gath_b,
    red_f,
    red_b,
    wgu,
    wdn,
    wgu_t,
    wdn_t,
    acc_f,
    acc_b,
    coef_g,
    coef_u,
    hbt,
    hid,
    dgu,
    dg,
    dg_in,
    pipe_send,
    pipe_recv,
    gs_f,
    gr_f,
    gs_b,
    gr_b,
    rs_f,
    rr_f,
    rs_b,
    rr_b,
    dp_send,
    dp_recv,
):
    width, rows = x_ref.shape
    units = wg_ref.shape[0]
    capacity = sgate_ref.shape[1]
    half = ring // 2
    groups = ring // GROUP
    me = lax.axis_index("expert")
    section = lax.axis_index("pipe")
    replica = lax.axis_index("dp")
    right, left = lax.rem(me + 1, ring), lax.rem(me + ring - 1, ring)
    ahead, behind = lax.rem(section + 1, sections), lax.rem(section + sections - 1, sections)
    peer = 1 - replica
    expert = me // (ring // EXPERTS)

    barrier = pltpu.get_barrier_semaphore()
    for axis, other in (
        ("expert", right),
        ("expert", left),
        ("pipe", ahead),
        ("pipe", behind),
        ("dp", peer),
    ):
        pl.semaphore_signal(barrier, inc=1, device_id={axis: other}, device_id_type=MESH)
    pl.semaphore_wait(barrier, 5)

    def shift(k):
        return pltpu.make_async_remote_copy(
            src_ref=(x_ref, c_ref)[k],
            dst_ref=(gath_f.at[me], craw)[k],
            send_sem=pipe_send.at[k],
            recv_sem=pipe_recv.at[k],
            device_id={"pipe": (ahead, behind)[k]},
            device_id_type=MESH,
        )

    shift(0).start()
    shift(1).start()

    def split_weights(g, carry):
        columns = pl.ds(pl.multiple_of(g * (GROUP * width), LANES), GROUP * width)
        both = jnp.concatenate([wg_ref[:, columns], wu_ref[:, columns]], axis=0)
        down = wd_ref[:, columns]
        for z in range(GROUP):
            piece = both[:, z * width : (z + 1) * width]
            wgu[GROUP * g + z] = piece
            wgu_t[GROUP * g + z] = jnp.transpose(piece)
            piece = down[:, z * width : (z + 1) * width]
            wdn[GROUP * g + z] = piece
            wdn_t[GROUP * g + z] = jnp.transpose(piece)
        return carry

    def gather_copy(stream, way, k, shard):
        buf, send, recv = ((gath_f, gs_f, gr_f), (gath_b, gs_b, gr_b))[stream]
        return pltpu.make_async_remote_copy(
            src_ref=buf.at[shard],
            dst_ref=buf.at[shard],
            send_sem=send.at[way, k],
            recv_sem=recv.at[way, k],
            device_id={"expert": (right, left)[way]},
            device_id_type=MESH,
        )

    def gather(stream, way, k):
        shard = lax.rem(me + ring - k, ring) if way == 0 else lax.rem(me + k, ring)
        return gather_copy(stream, way, k, shard)

    def arrived(stream, way, k):
        shard = lax.rem(me + ring - 1 - k, ring) if way == 0 else lax.rem(me + 1 + k, ring)
        gather_copy(stream, way, k, shard).wait_recv()
        return shard

    def use_f(shard):
        acc_f[...] += dot(wgu[shard], gath_f[shard])

    def use_b(shard):
        acc_b[...] += dot(wdn[shard], gath_b[shard])

    acc_f[...] = jnp.zeros_like(acc_f)
    acc_b[...] = jnp.zeros_like(acc_b)

    shift(0).wait_recv()
    gather(0, 0, 0).start()
    gather(0, 1, 0).start()
    shift(1).wait_recv()
    gath_b[me] = (craw[...].astype(F32) * bweight_ref[...].astype(F32)).astype(BF16)
    gather(1, 0, 0).start()
    gather(1, 1, 0).start()

    lax.fori_loop(0, groups, split_weights, 0)

    before = (
        lax.broadcasted_iota(jnp.int32, (rows, rows), 0)
        < lax.broadcasted_iota(jnp.int32, (rows, rows), 1)
    ).astype(F32).astype(BF16)
    named = jnp.broadcast_to((broute_ref[...] == expert).astype(F32), (capacity, rows))
    slot = dot(named.astype(BF16), before)
    column = lax.broadcasted_iota(jnp.int32, (capacity, rows), 0).astype(F32)
    place = jnp.where(slot == column, named, 0.0).astype(BF16)
    gate_b = dot(sgate_ref[...], place)
    upper_b = dot(sup_ref[...], place)
    sig = jax.nn.sigmoid(gate_b)
    coef_g[...] = upper_b * sig * (1.0 + gate_b * (1.0 - sig))
    coef_u[...] = gate_b * sig
    hbt[...] = (gate_b * sig * upper_b).astype(BF16)

    use_f(me)
    use_b(me)

    def gather_both(k, carry):
        for stream, use in ((0, use_f), (1, use_b)):
            one = arrived(stream, 0, k)
            gather(stream, 0, k + 1).start()
            two = arrived(stream, 1, k)

            @pl.when(k < half - 2)
            def _():
                gather(stream, 1, k + 1).start()

            use(one)
            use(two)
        return carry

    lax.fori_loop(0, half - 1, gather_both, 0)
    use_f(arrived(0, 0, half - 1))
    gate = acc_f[:units]
    upper = acc_f[units:]
    hid[...] = jnp.where(
        froute_ref[...] == expert, gate * jax.nn.sigmoid(gate) * upper, 0.0
    ).astype(BF16)

    def part_f(shard):
        return dot(wdn_t[shard], hid[...])

    def part_b(shard):
        return dot(wgu_t[shard], dgu[...])

    def reduce(stream, way, k):
        buf, send, recv = ((red_f, rs_f, rr_f), (red_b, rs_b, rr_b))[stream]
        return pltpu.make_async_remote_copy(
            src_ref=buf.at[way, k],
            dst_ref=buf.at[way, k + 1],
            send_sem=send.at[way, k],
            recv_sem=recv.at[way, k],
            device_id={"expert": (right, left)[way]},
            device_id_type=MESH,
        )

    def target(way, k):
        return lax.rem(me + half - k + ring, ring) if way == 0 else lax.rem(me + ring - half + 1 + k, ring)

    for way in range(2):
        red_f[way, 0] = part_f(target(way, 0)).astype(BF16)
        reduce(0, way, 0).start()

    use_b(arrived(1, 0, half - 1))
    d_hidden = acc_b[...]
    dgu[:units] = (d_hidden * coef_g[...]).astype(BF16)
    dgu[units:] = (d_hidden * coef_u[...]).astype(BF16)
    for way in range(2):
        red_b[way, 0] = part_b(target(way, 0)).astype(BF16)
        reduce(1, way, 0).start()

    def down_piece(g):
        shards = gath_b[pl.ds(GROUP * g, GROUP)].reshape(GROUP * width, rows)
        start = pl.multiple_of(g * (GROUP * width), LANES)
        dg[:, pl.ds(start, GROUP * width)] = dot_t(hbt[...], shards)

    def reduce_step(k):
        for stream, part in ((0, part_f), (1, part_b)):
            buf = (red_f, red_b)[stream]
            term = part(target(0, k))
            reduce(stream, 0, k - 1).wait_recv()
            buf[0, k] = (buf[0, k].astype(F32) + term).astype(BF16)
            reduce(stream, 0, k).start()

            @pl.when(k < half - 1)
            def _():
                term = part(target(1, k))
                reduce(stream, 1, k - 1).wait_recv()
                buf[1, k] = (buf[1, k].astype(F32) + term).astype(BF16)
                reduce(stream, 1, k).start()

    def early(k, carry):
        reduce_step(k)
        down_piece(k - 1)
        return carry

    def late(k, carry):
        reduce_step(k)
        return carry

    def give():
        return pltpu.make_async_remote_copy(
            src_ref=dg.at[pl.ds(pl.multiple_of(peer * (units // 2), 8), units // 2)],
            dst_ref=dg_in,
            send_sem=dp_send,
            recv_sem=dp_recv,
            device_id={"dp": peer},
            device_id_type=MESH,
        )

    lax.fori_loop(1, groups + 1, early, 0)
    give().start()
    lax.fori_loop(groups + 1, half, late, 0)

    give().wait_recv()
    mine_rows = pl.ds(pl.multiple_of(replica * (units // 2), 8), units // 2)
    dgrad_ref[...] = dg[mine_rows, :] + dg_in[...]

    for stream, part in ((0, part_f), (1, part_b)):
        buf = (red_f, red_b)[stream]
        total = part(me)
        reduce(stream, 1, half - 2).wait_recv()
        total = total + buf[1, half - 1].astype(F32)
        reduce(stream, 0, half - 1).wait_recv()
        total = total + buf[0, half].astype(F32)
        summed = total.astype(BF16).astype(F32)
        if stream == 0:
            fout_ref[...] = (
                gath_f[me].astype(F32) + fweight_ref[...].astype(F32) * summed
            ).astype(BF16)
        else:
            bout_ref[...] = (craw[...].astype(F32) + summed).astype(BF16)

    shift(0).wait_send()
    shift(1).wait_send()
    give().wait_send()
    for stream in range(2):
        for way, count in ((0, half), (1, half - 1)):

            def drain(k, carry):
                gather(stream, way, k).wait_send()
                reduce(stream, way, k).wait_send()
                return carry

            lax.fori_loop(0, count, drain, 0)


def solution(mesh):
    ring = mesh.shape["expert"]
    sections = mesh.shape["pipe"]
    half = ring // 2

    def body(
        fwd_sent,
        fwd_route,
        fwd_weight,
        bwd_cot,
        bwd_route,
        bwd_weight,
        saved_gate,
        saved_up,
        gate_weight,
        up_weight,
        down_weight,
    ):
        rows, width = fwd_sent.shape[1:]
        units, model = gate_weight.shape[1:]
        dma = pltpu.SemaphoreType.DMA
        vmem = pl.BlockSpec(memory_space=pltpu.VMEM)
        outs = pl.pallas_call(
            functools.partial(kernel, ring, sections),
            out_shape=(
                jax.ShapeDtypeStruct((width, rows), BF16),
                jax.ShapeDtypeStruct((width, rows), BF16),
                jax.ShapeDtypeStruct((units // 2, model), F32),
            ),
            in_specs=[vmem] * 11,
            out_specs=(vmem,) * 3,
            scratch_shapes=[
                pltpu.VMEM((width, rows), BF16),
                pltpu.VMEM((ring, width, rows), BF16),
                pltpu.VMEM((ring, width, rows), BF16),
                pltpu.VMEM((2, half + 1, width, rows), BF16),
                pltpu.VMEM((2, half + 1, width, rows), BF16),
                pltpu.VMEM((ring, 2 * units, width), BF16),
                pltpu.VMEM((ring, units, width), BF16),
                pltpu.VMEM((ring, width, 2 * units), BF16),
                pltpu.VMEM((ring, width, units), BF16),
                pltpu.VMEM((2 * units, rows), F32),
                pltpu.VMEM((units, rows), F32),
                pltpu.VMEM((units, rows), F32),
                pltpu.VMEM((units, rows), F32),
                pltpu.VMEM((units, rows), BF16),
                pltpu.VMEM((units, rows), BF16),
                pltpu.VMEM((2 * units, rows), BF16),
                pltpu.VMEM((units, model), F32),
                pltpu.VMEM((units // 2, model), F32),
                dma((2,)),
                dma((2,)),
            ]
            + [dma((2, half))] * 8
            + [dma, dma],
            compiler_params=pltpu.CompilerParams(
                collective_id=0, has_side_effects=True, vmem_limit_bytes=56 * 1024 * 1024
            ),
        )(
            fwd_sent[0].T,
            fwd_route[0].T,
            fwd_weight[0].T,
            bwd_cot[0].T,
            bwd_route[0].T,
            bwd_weight[0].T,
            saved_gate[0, 0].T,
            saved_up[0, 0].T,
            gate_weight[0],
            up_weight[0],
            down_weight[0],
        )
        return outs[0].T[None], outs[1].T[None], outs[2][None]

    in_specs = (
        P("pipe", "dp", "expert"),
        P("pipe", "dp", None),
        P("pipe", "dp", None),
        P("pipe", "dp", "expert"),
        P("pipe", "dp", None),
        P("pipe", "dp", None),
        P("pipe", "dp", None, "expert"),
        P("pipe", "dp", None, "expert"),
        P("pipe", "expert", None),
        P("pipe", "expert", None),
        P("pipe", "expert", None),
    )
    out_specs = (
        P("pipe", "dp", "expert"),
        P("pipe", "dp", "expert"),
        P("pipe", ("expert", "dp"), None),
    )
    return jax.shard_map(body, mesh=mesh, in_specs=in_specs, out_specs=out_specs, check_vma=False)
```

time: 207 us -> 196 us (0.947)
  local copies, waits for them, and re-layouts: 12.2 us -> 4.4 us
    unnamed x23 -> x5, local copies, waits for them, and re-layouts: 9.13 us -> 4.4 us
    squeeze x4 -> x0, local copies, waits for them, and re-layouts: 3.11 us -> none  [the longest x1 0.8 us: body(): bwd_route[0]]
    pallas_call x1, Pallas kernels: 193 us -> 191 us  [body(): pl.pallas_call(functools.partial(kernel, ring, sections), out_shape=(jax....]
where the time goes in v2:
time: 196 us
  Pallas kernels  191 us (97%)
  local copies, waits for them, and re-layouts  4.4 us (2%)
    pallas_call x1, Pallas kernels, body(): pl.pallas_call(functools.partial(kernel, ring, sections), out_shape=(jax....  191 us
    unnamed x5, local copies, waits for them, and re-layouts  4.4 us

profile of v2, /device:TPU:24, one launch (start us, length us, event | category | flops | bytes accessed | tf_op | source)
XLA Modules:
  0.0 195.8 jit_solution(17092547530382156606)
XLA Ops:
  0.6 190.7 %shard_map.130 = (bf16[224,256]{1,0:T(8,128)(2,1)}, bf16[224,256]{1,0:T(8,128)(2,1)}, f32[32,7168]{1,0:T(8,128)}) custom-call(bf16[224,256]{1,0:T(8,128)(2,1)} %bitcast.32, s32[1,256]{1,0:T(1,128)} %bitcast.36, bf16[1,256]{1,0:T(2,128)(2,1)} %bitcast.37, bf16[224,256]{1,0:T(8,128)(2,1)} %bitcast.33, s32[1,256]{1,0:T(1,128)} %bitcast.38, ...), custom_call_target="tpu_custom_call" | custom-call | tf_op jit(solution)/shard_map/pallas_call | solution.py:334
  191.4 0.0 copy-start
  191.4 1.6 copy.17
  193.0 0.0 copy-done
  193.0 0.6 copy.18
  193.6 2.2 %copy.19 = f32[1,32,7168]{2,1,0:T(8,128)} copy(f32[1,32,7168]{2,1,0:T(8,128)} %bitcast.26) | data formatting | bytes 1835008
Async XLA Ops:
  191.4 1.6 copy-start

commit v3 on v2

--- a/solution.py
+++ b/solution.py
@@ -41,7 +41,6 @@
     fout_ref,
     bout_ref,
     dgrad_ref,
-    craw,
     gath_f,
     gath_b,
     red_f,
@@ -61,14 +60,10 @@
     dg_in,
     pipe_send,
     pipe_recv,
-    gs_f,
-    gr_f,
-    gs_b,
-    gr_b,
-    rs_f,
-    rr_f,
-    rs_b,
-    rr_b,
+    gs,
+    gr,
+    rs,
+    rr,
     dp_send,
     dp_recv,
 ):
@@ -85,29 +80,49 @@
     peer = 1 - replica
     expert = me // (ring // EXPERTS)
 
+    part_width = width // 2
+    hops = ((half, half - 1), (half - 1, half))
+    flows = [(stream, h) for h in range(2) for stream in range(2)]
+    sides = (right, left)
+    stage = (ahead, behind)
+
     barrier = pltpu.get_barrier_semaphore()
-    for axis, other in (
-        ("expert", right),
-        ("expert", left),
-        ("pipe", ahead),
-        ("pipe", behind),
-        ("dp", peer),
-    ):
-        pl.semaphore_signal(barrier, inc=1, device_id={axis: other}, device_id_type=MESH)
-    pl.semaphore_wait(barrier, 5)
-
-    def shift(k):
+    partners = [{"expert": right}, {"expert": left}, {"dp": peer}]
+    for section_to in stage:
+        partners.append({"pipe": section_to})
+        partners += [{"pipe": section_to, "expert": side} for side in sides]
+    for partner in partners:
+        pl.semaphore_signal(barrier, inc=1, device_id=partner, device_id_type=MESH)
+    pl.semaphore_wait(barrier, len(partners))
+
+    def band(h):
+        return pl.ds(h * part_width, part_width)
+
+    def shift(stream):
         return pltpu.make_async_remote_copy(
-            src_ref=(x_ref, c_ref)[k],
-            dst_ref=(gath_f.at[me], craw)[k],
-            send_sem=pipe_send.at[k],
-            recv_sem=pipe_recv.at[k],
-            device_id={"pipe": (ahead, behind)[k]},
+            src_ref=(x_ref, c_ref)[stream],
+            dst_ref=(gath_f, gath_b)[stream].at[me],
+            send_sem=pipe_send.at[stream],
+            recv_sem=pipe_recv.at[stream],
+            device_id={"pipe": stage[stream]},
             device_id_type=MESH,
         )
 
-    shift(0).start()
-    shift(1).start()
+    def first(stream, h, way):
+        return pltpu.make_async_remote_copy(
+            src_ref=(x_ref, c_ref)[stream].at[band(h)],
+            dst_ref=(gath_f, gath_b)[stream].at[me, band(h)],
+            send_sem=gs.at[stream, h, way, 0],
+            recv_sem=gr.at[stream, h, way, 0],
+            device_id={"pipe": stage[stream], "expert": sides[way]},
+            device_id_type=MESH,
+        )
+
+    for stream, h in flows:
+        for way in range(2):
+            first(stream, h, way).start()
+    for stream in range(2):
+        shift(stream).start()
 
     def split_weights(g, carry):
         columns = pl.ds(pl.multiple_of(g * (GROUP * width), LANES), GROUP * width)
@@ -122,42 +137,37 @@
             wdn_t[GROUP * g + z] = jnp.transpose(piece)
         return carry
 
-    def gather_copy(stream, way, k, shard):
-        buf, send, recv = ((gath_f, gs_f, gr_f), (gath_b, gs_b, gr_b))[stream]
+    def gather_copy(stream, h, way, k, shard):
+        piece = (gath_f, gath_b)[stream].at[shard, band(h)]
         return pltpu.make_async_remote_copy(
-            src_ref=buf.at[shard],
-            dst_ref=buf.at[shard],
-            send_sem=send.at[way, k],
-            recv_sem=recv.at[way, k],
-            device_id={"expert": (right, left)[way]},
+            src_ref=piece,
+            dst_ref=piece,
+            send_sem=gs.at[stream, h, way, k],
+            recv_sem=gr.at[stream, h, way, k],
+            device_id={"expert": sides[way]},
             device_id_type=MESH,
         )
 
-    def gather(stream, way, k):
-        shard = lax.rem(me + ring - k, ring) if way == 0 else lax.rem(me + k, ring)
-        return gather_copy(stream, way, k, shard)
-
-    def arrived(stream, way, k):
-        shard = lax.rem(me + ring - 1 - k, ring) if way == 0 else lax.rem(me + 1 + k, ring)
-        gather_copy(stream, way, k, shard).wait_recv()
-        return shard
+    def source(way, k):
+        return lax.rem(me + ring - 1 - k, ring) if way == 0 else lax.rem(me + 1 + k, ring)
+
+    def arrived(stream, h, way, k):
+        gather_copy(stream, h, way, k, source(way, k)).wait_recv()
+
+    def forward(stream, h, way, k):
+        return gather_copy(stream, h, way, k + 1, source(way, k))
+
+    bweight = bweight_ref[...].astype(F32)
 
     def use_f(shard):
         acc_f[...] += dot(wgu[shard], gath_f[shard])
 
     def use_b(shard):
-        acc_b[...] += dot(wdn[shard], gath_b[shard])
+        cot = (gath_b[shard].astype(F32) * bweight).astype(BF16)
+        acc_b[...] += dot(wdn[shard], cot)
 
     acc_f[...] = jnp.zeros_like(acc_f)
     acc_b[...] = jnp.zeros_like(acc_b)
-
-    shift(0).wait_recv()
-    gather(0, 0, 0).start()
-    gather(0, 1, 0).start()
-    shift(1).wait_recv()
-    gath_b[me] = (craw[...].astype(F32) * bweight_ref[...].astype(F32)).astype(BF16)
-    gather(1, 0, 0).start()
-    gather(1, 1, 0).start()
 
     lax.fori_loop(0, groups, split_weights, 0)
 
@@ -176,82 +186,96 @@
     coef_u[...] = gate_b * sig
     hbt[...] = (gate_b * sig * upper_b).astype(BF16)
 
+    shift(0).wait_recv()
     use_f(me)
+    shift(1).wait_recv()
     use_b(me)
 
-    def gather_both(k, carry):
-        for stream, use in ((0, use_f), (1, use_b)):
-            one = arrived(stream, 0, k)
-            gather(stream, 0, k + 1).start()
-            two = arrived(stream, 1, k)
-
-            @pl.when(k < half - 2)
-            def _():
-                gather(stream, 1, k + 1).start()
-
-            use(one)
-            use(two)
+    def gather_all(k, carry):
+        for stream, h in flows:
+            for way in range(2):
+                arrived(stream, h, way, k)
+                if hops[h][way] == half:
+                    forward(stream, h, way, k).start()
+                else:
+
+                    @pl.when(k < half - 2)
+                    def _():
+                        forward(stream, h, way, k).start()
+
+            if h == 1:
+                for way in range(2):
+                    (use_f, use_b)[stream](source(way, k))
         return carry
 
-    lax.fori_loop(0, half - 1, gather_both, 0)
-    use_f(arrived(0, 0, half - 1))
+    lax.fori_loop(0, half - 1, gather_all, 0)
+    for h in range(2):
+        arrived(0, h, h, half - 1)
+    use_f(source(0, half - 1))
     gate = acc_f[:units]
     upper = acc_f[units:]
     hid[...] = jnp.where(
         froute_ref[...] == expert, gate * jax.nn.sigmoid(gate) * upper, 0.0
     ).astype(BF16)
 
-    def part_f(shard):
-        return dot(wdn_t[shard], hid[...])
-
-    def part_b(shard):
-        return dot(wgu_t[shard], dgu[...])
-
-    def reduce(stream, way, k):
-        buf, send, recv = ((red_f, rs_f, rr_f), (red_b, rs_b, rr_b))[stream]
+    def part(stream, h, shard):
+        if stream == 0:
+            return dot(wdn_t[shard, band(h)], hid[...])
+        return dot(wgu_t[shard, band(h)], dgu[...])
+
+    def reduce(stream, h, way, k):
+        buf = (red_f, red_b)[stream]
         return pltpu.make_async_remote_copy(
-            src_ref=buf.at[way, k],
-            dst_ref=buf.at[way, k + 1],
-            send_sem=send.at[way, k],
-            recv_sem=recv.at[way, k],
-            device_id={"expert": (right, left)[way]},
+            src_ref=buf.at[h, way, k],
+            dst_ref=buf.at[h, way, k + 1],
+            send_sem=rs.at[stream, h, way, k],
+            recv_sem=rr.at[stream, h, way, k],
+            device_id={"expert": sides[way]},
             device_id_type=MESH,
         )
 
-    def target(way, k):
-        return lax.rem(me + half - k + ring, ring) if way == 0 else lax.rem(me + ring - half + 1 + k, ring)
-
-    for way in range(2):
-        red_f[way, 0] = part_f(target(way, 0)).astype(BF16)
-        reduce(0, way, 0).start()
-
-    use_b(arrived(1, 0, half - 1))
+    def target(h, way, k):
+        ahead_by = hops[h][way] - k
+        return lax.rem(me + (ahead_by if way == 0 else ring - ahead_by), ring)
+
+    def begin(stream):
+        for h in range(2):
+            for way in range(2):
+                (red_f, red_b)[stream][h, way, 0] = part(stream, h, target(h, way, 0)).astype(BF16)
+                reduce(stream, h, way, 0).start()
+
+    begin(0)
+    for h in range(2):
+        arrived(1, h, h, half - 1)
+    use_b(source(0, half - 1))
     d_hidden = acc_b[...]
     dgu[:units] = (d_hidden * coef_g[...]).astype(BF16)
     dgu[units:] = (d_hidden * coef_u[...]).astype(BF16)
-    for way in range(2):
-        red_b[way, 0] = part_b(target(way, 0)).astype(BF16)
-        reduce(1, way, 0).start()
+    begin(1)
 
     def down_piece(g):
-        shards = gath_b[pl.ds(GROUP * g, GROUP)].reshape(GROUP * width, rows)
+        raw = gath_b[pl.ds(GROUP * g, GROUP)].reshape(GROUP * width, rows)
+        shards = (raw.astype(F32) * bweight).astype(BF16)
         start = pl.multiple_of(g * (GROUP * width), LANES)
         dg[:, pl.ds(start, GROUP * width)] = dot_t(hbt[...], shards)
 
+    def relay(stream, h, way, k):
+        buf = (red_f, red_b)[stream]
+        term = part(stream, h, target(h, way, k))
+        reduce(stream, h, way, k - 1).wait_recv()
+        buf[h, way, k] = (buf[h, way, k].astype(F32) + term).astype(BF16)
+        reduce(stream, h, way, k).start()
+
     def reduce_step(k):
-        for stream, part in ((0, part_f), (1, part_b)):
-            buf = (red_f, red_b)[stream]
-            term = part(target(0, k))
-            reduce(stream, 0, k - 1).wait_recv()
-            buf[0, k] = (buf[0, k].astype(F32) + term).astype(BF16)
-            reduce(stream, 0, k).start()
-
-            @pl.when(k < half - 1)
-            def _():
-                term = part(target(1, k))
-                reduce(stream, 1, k - 1).wait_recv()
-                buf[1, k] = (buf[1, k].astype(F32) + term).astype(BF16)
-                reduce(stream, 1, k).start()
+        for stream, h in flows:
+            for way in range(2):
+                if hops[h][way] == half:
+                    relay(stream, h, way, k)
+                else:
+
+                    @pl.when(k < half - 1)
+                    def _():
+                        relay(stream, h, way, k)
 
     def early(k, carry):
         reduce_step(k)
@@ -280,33 +304,34 @@
     mine_rows = pl.ds(pl.multiple_of(replica * (units // 2), 8), units // 2)
     dgrad_ref[...] = dg[mine_rows, :] + dg_in[...]
 
-    for stream, part in ((0, part_f), (1, part_b)):
+    for stream, h in flows:
         buf = (red_f, red_b)[stream]
-        total = part(me)
-        reduce(stream, 1, half - 2).wait_recv()
-        total = total + buf[1, half - 1].astype(F32)
-        reduce(stream, 0, half - 1).wait_recv()
-        total = total + buf[0, half].astype(F32)
+        total = part(stream, h, me)
+        for way in (1 - h, h):
+            last = hops[h][way]
+            reduce(stream, h, way, last - 1).wait_recv()
+            total = total + buf[h, way, last].astype(F32)
         summed = total.astype(BF16).astype(F32)
         if stream == 0:
-            fout_ref[...] = (
-                gath_f[me].astype(F32) + fweight_ref[...].astype(F32) * summed
-            ).astype(BF16)
+            own = gath_f[me, band(h)].astype(F32)
+            fout_ref[band(h)] = (own + fweight_ref[...].astype(F32) * summed).astype(BF16)
         else:
-            bout_ref[...] = (craw[...].astype(F32) + summed).astype(BF16)
+            bout_ref[band(h)] = (gath_b[me, band(h)].astype(F32) + summed).astype(BF16)
 
     shift(0).wait_send()
     shift(1).wait_send()
     give().wait_send()
-    for stream in range(2):
-        for way, count in ((0, half), (1, half - 1)):
+    for stream, h in flows:
+        for way in range(2):
+            first(stream, h, way).wait_send()
+            reduce(stream, h, way, 0).wait_send()
 
             def drain(k, carry):
-                gather(stream, way, k).wait_send()
-                reduce(stream, way, k).wait_send()
+                gather_copy(stream, h, way, k, me).wait_send()
+                reduce(stream, h, way, k).wait_send()
                 return carry
 
-            lax.fori_loop(0, count, drain, 0)
+            lax.fori_loop(1, hops[h][way], drain, 0)
 
 
 def solution(mesh):
@@ -341,11 +366,10 @@
             in_specs=[vmem] * 11,
             out_specs=(vmem,) * 3,
             scratch_shapes=[
-                pltpu.VMEM((width, rows), BF16),
                 pltpu.VMEM((ring, width, rows), BF16),
                 pltpu.VMEM((ring, width, rows), BF16),
-                pltpu.VMEM((2, half + 1, width, rows), BF16),
-                pltpu.VMEM((2, half + 1, width, rows), BF16),
+                pltpu.VMEM((2, 2, half + 1, width // 2, rows), BF16),
+                pltpu.VMEM((2, 2, half + 1, width // 2, rows), BF16),
                 pltpu.VMEM((ring, 2 * units, width), BF16),
                 pltpu.VMEM((ring, units, width), BF16),
                 pltpu.VMEM((ring, width, 2 * units), BF16),
@@ -362,7 +386,7 @@
                 dma((2,)),
                 dma((2,)),
             ]
-            + [dma((2, half))] * 8
+            + [dma((2, 2, 2, half))] * 4
             + [dma, dma],
             compiler_params=pltpu.CompilerParams(
                 collective_id=0, has_side_effects=True, vmem_limit_bytes=56 * 1024 * 1024

time: 196 us -> 191 us (0.974)
  Pallas kernels: 191 us -> 186 us
    pallas_call x1, Pallas kernels: 191 us -> 186 us  [body(): pl.pallas_call(functools.partial(kernel, ring, sections), out_shape=(jax....]
where the time goes in v3:
time: 191 us
  Pallas kernels  186 us (97%)
  local copies, waits for them, and re-layouts  4.4 us (2%)
    pallas_call x1, Pallas kernels, body(): pl.pallas_call(functools.partial(kernel, ring, sections), out_shape=(jax....  186 us
    unnamed x5, local copies, waits for them, and re-layouts  4.4 us

profile of v3, /device:TPU:24, one launch (start us, length us, event | category | flops | bytes accessed | tf_op | source)
XLA Modules:
  0.0 190.7 jit_solution(14388169333436118237)
XLA Ops:
  0.6 185.7 %shard_map.130 = (bf16[224,256]{1,0:T(8,128)(2,1)}, bf16[224,256]{1,0:T(8,128)(2,1)}, f32[32,7168]{1,0:T(8,128)}) custom-call(bf16[224,256]{1,0:T(8,128)(2,1)} %bitcast.32, s32[1,256]{1,0:T(1,128)} %bitcast.36, bf16[1,256]{1,0:T(2,128)(2,1)} %bitcast.37, bf16[224,256]{1,0:T(8,128)(2,1)} %bitcast.33, s32[1,256]{1,0:T(1,128)} %bitcast.38, ...), custom_call_target="tpu_custom_call" | custom-call | tf_op jit(solution)/shard_map/pallas_call | solution.py:359
  186.3 0.0 copy-start
  186.3 1.6 copy.17
  187.9 0.0 copy-done
  187.9 0.6 copy.18
  188.6 2.2 %copy.19 = f32[1,32,7168]{2,1,0:T(8,128)} copy(f32[1,32,7168]{2,1,0:T(8,128)} %bitcast.26) | data formatting | bytes 1835008
Async XLA Ops:
  186.3 1.6 copy-start

commit v4 on v3

--- a/solution.py
+++ b/solution.py
@@ -35,12 +35,16 @@
     bweight_ref,
     sgate_ref,
     sup_ref,
+    wg_hbm,
+    wu_hbm,
+    wd_hbm,
+    fout_ref,
+    bout_ref,
+    own_ref,
+    peer_ref,
     wg_ref,
     wu_ref,
     wd_ref,
-    fout_ref,
-    bout_ref,
-    dgrad_ref,
     gath_f,
     gath_b,
     red_f,
@@ -57,7 +61,8 @@
     hid,
     dgu,
     dg,
-    dg_in,
+    load_sem,
+    keep_sem,
     pipe_send,
     pipe_recv,
     gs,
@@ -86,6 +91,13 @@
     sides = (right, left)
     stage = (ahead, behind)
 
+    loads = [
+        pltpu.make_async_copy(hbm, ref, load_sem.at[i])
+        for i, (hbm, ref) in enumerate(((wg_hbm, wg_ref), (wu_hbm, wu_ref), (wd_hbm, wd_ref)))
+    ]
+    for load in loads:
+        load.start()
+
     barrier = pltpu.get_barrier_semaphore()
     partners = [{"expert": right}, {"expert": left}, {"dp": peer}]
     for section_to in stage:
@@ -124,7 +136,7 @@
     for stream in range(2):
         shift(stream).start()
 
-    def split_weights(g, carry):
+    def split_weights(g):
         columns = pl.ds(pl.multiple_of(g * (GROUP * width), LANES), GROUP * width)
         both = jnp.concatenate([wg_ref[:, columns], wu_ref[:, columns]], axis=0)
         down = wd_ref[:, columns]
@@ -135,7 +147,6 @@
             piece = down[:, z * width : (z + 1) * width]
             wdn[GROUP * g + z] = piece
             wdn_t[GROUP * g + z] = jnp.transpose(piece)
-        return carry
 
     def gather_copy(stream, h, way, k, shard):
         piece = (gath_f, gath_b)[stream].at[shard, band(h)]
@@ -168,8 +179,6 @@
 
     acc_f[...] = jnp.zeros_like(acc_f)
     acc_b[...] = jnp.zeros_like(acc_b)
-
-    lax.fori_loop(0, groups, split_weights, 0)
 
     before = (
         lax.broadcasted_iota(jnp.int32, (rows, rows), 0)
@@ -186,29 +195,53 @@
     coef_u[...] = gate_b * sig
     hbt[...] = (gate_b * sig * upper_b).astype(BF16)
 
+    def pass_on(stream, h, k):
+        for way in range(2):
+            arrived(stream, h, way, k)
+            if hops[h][way] == half:
+                forward(stream, h, way, k).start()
+            else:
+
+                @pl.when(k < half - 2)
+                def _():
+                    forward(stream, h, way, k).start()
+
+    def use(k):
+        for way in range(2):
+            use_f(source(way, k))
+            use_b(source(way, k))
+
+    both = 2 - groups % 2
+    opening = groups // both
+
+    def gather_first(k, carry):
+        for stream, h in flows:
+            pass_on(stream, h, k)
+            if stream == 1 and h < both:
+                split_weights(both * k + h)
+        return carry
+
+    def gather_rest(k, carry):
+        for stream, h in flows:
+            pass_on(stream, h, k)
+
+        @pl.when(k < 2 * opening)
+        def _():
+            use(k - opening)
+
+        use(k)
+        return carry
+
+    for load in loads:
+        load.wait()
+    lax.fori_loop(0, opening, gather_first, 0)
     shift(0).wait_recv()
     use_f(me)
     shift(1).wait_recv()
     use_b(me)
-
-    def gather_all(k, carry):
-        for stream, h in flows:
-            for way in range(2):
-                arrived(stream, h, way, k)
-                if hops[h][way] == half:
-                    forward(stream, h, way, k).start()
-                else:
-
-                    @pl.when(k < half - 2)
-                    def _():
-                        forward(stream, h, way, k).start()
-
-            if h == 1:
-                for way in range(2):
-                    (use_f, use_b)[stream](source(way, k))
-        return carry
-
-    lax.fori_loop(0, half - 1, gather_all, 0)
+    lax.fori_loop(opening, half - 1, gather_rest, 0)
+    for k in range(half - 1 - opening, opening):
+        use(k)
     for h in range(2):
         arrived(0, h, h, half - 1)
     use_f(source(0, half - 1))
@@ -289,20 +322,20 @@
     def give():
         return pltpu.make_async_remote_copy(
             src_ref=dg.at[pl.ds(pl.multiple_of(peer * (units // 2), 8), units // 2)],
-            dst_ref=dg_in,
+            dst_ref=peer_ref,
             send_sem=dp_send,
             recv_sem=dp_recv,
             device_id={"dp": peer},
             device_id_type=MESH,
         )
 
+    mine_rows = pl.ds(pl.multiple_of(replica * (units // 2), 8), units // 2)
+    keep = pltpu.make_async_copy(dg.at[mine_rows], own_ref, keep_sem)
+
     lax.fori_loop(1, groups + 1, early, 0)
     give().start()
+    keep.start()
     lax.fori_loop(groups + 1, half, late, 0)
-
-    give().wait_recv()
-    mine_rows = pl.ds(pl.multiple_of(replica * (units // 2), 8), units // 2)
-    dgrad_ref[...] = dg[mine_rows, :] + dg_in[...]
 
     for stream, h in flows:
         buf = (red_f, red_b)[stream]
@@ -321,6 +354,8 @@
     shift(0).wait_send()
     shift(1).wait_send()
     give().wait_send()
+    give().wait_recv()
+    keep.wait()
     for stream, h in flows:
         for way in range(2):
             first(stream, h, way).wait_send()
@@ -356,16 +391,21 @@
         units, model = gate_weight.shape[1:]
         dma = pltpu.SemaphoreType.DMA
         vmem = pl.BlockSpec(memory_space=pltpu.VMEM)
+        anywhere = pl.BlockSpec(memory_space=pl.ANY)
         outs = pl.pallas_call(
             functools.partial(kernel, ring, sections),
             out_shape=(
                 jax.ShapeDtypeStruct((width, rows), BF16),
                 jax.ShapeDtypeStruct((width, rows), BF16),
                 jax.ShapeDtypeStruct((units // 2, model), F32),
+                jax.ShapeDtypeStruct((units // 2, model), F32),
             ),
-            in_specs=[vmem] * 11,
-            out_specs=(vmem,) * 3,
+            in_specs=[vmem] * 8 + [anywhere] * 3,
+            out_specs=(vmem,) * 2 + (anywhere,) * 2,
             scratch_shapes=[
+                pltpu.VMEM((units, model), BF16),
+                pltpu.VMEM((units, model), BF16),
+                pltpu.VMEM((units, model), BF16),
                 pltpu.VMEM((ring, width, rows), BF16),
                 pltpu.VMEM((ring, width, rows), BF16),
                 pltpu.VMEM((2, 2, half + 1, width // 2, rows), BF16),
@@ -382,7 +422,8 @@
                 pltpu.VMEM((units, rows), BF16),
                 pltpu.VMEM((2 * units, rows), BF16),
                 pltpu.VMEM((units, model), F32),
-                pltpu.VMEM((units // 2, model), F32),
+                dma((3,)),
+                dma,
                 dma((2,)),
                 dma((2,)),
             ]
@@ -404,7 +445,7 @@
             up_weight[0],
             down_weight[0],
         )
-        return outs[0].T[None], outs[1].T[None], outs[2][None]
+        return outs[0].T[None], outs[1].T[None], (outs[2] + outs[3])[None]
 
     in_specs = (
         P("pipe", "dp", "expert"),

time: 191 us -> 190 us (level)
  local copies, waits for them, and re-layouts: 4.4 us -> 1.59 us
  other arithmetic: 0 us -> 2.5 us
  Pallas kernels: 186 us -> 184 us
    unnamed x5 -> x6, local copies, waits for them, and re-layouts: 4.4 us -> 1.59 us
    broadcast_in_dim x0 -> x1, other arithmetic: none -> 2.5 us  [body(): return (outs[0].T[None], outs[1].T[None], (outs[2] + outs[3])[None])]
where the time goes in v4:
time: 190 us; the launch traced here: 189 us
  Pallas kernels  184 us (97%)
  other arithmetic  2.5 us (1%)
    pallas_call x1, Pallas kernels, body(): pl.pallas_call(functools.partial(kernel, ring, sections), out_shape=(jax....  184 us

profile of v4, /device:TPU:24, one launch (start us, length us, event | category | flops | bytes accessed | tf_op | source)
XLA Modules:
  0.0 189.1 jit_solution(6199542321449952848)
XLA Ops:
  0.6 184.3 %shard_map.130 = (bf16[224,256]{1,0:T(8,128)(2,1)}, bf16[224,256]{1,0:T(8,128)(2,1)}, f32[32,7168]{1,0:T(8,128)}, f32[32,7168]{1,0:T(8,128)}) custom-call(bf16[224,256]{1,0:T(8,128)(2,1)} %bitcast.32, s32[1,256]{1,0:T(1,128)} %bitcast.36, bf16[1,256]{1,0:T(2,128)(2,1)} %bitcast.37, bf16[224,256]{1,0:T(8,128)(2,1)} %bitcast.33, s32[1,256]{1,0:T(1,128)} %bitcast.38, ...), custom_call_target="tpu_custom_call" | custom-call | tf_op jit(solution)/shard_map/pallas_call | solution.py:395
  185.0 0.0 copy-start.1
  185.0 2.5 %add_bitcast_fusion = f32[1,32,7168]{2,1,0:T(8,128)} fusion(f32[32,7168]{1,0:T(8,128)} %get-tuple-element.9, f32[32,7168]{1,0:T(8,128)} %get-tuple-element.10), kind=kLoop, calls=%fused_computation | loop fusion | flops 229376 | bytes 2752512 | tf_op jit(solution)/shard_map/broadcast_in_dim | solution.py:448
  187.5 0.0 copy-done.1
  187.5 0.0 copy-start
  187.5 0.6 copy.16
  188.1 0.3 copy-done
  188.4 0.6 copy.17
Async XLA Ops:
  185.0 2.5 %copy-start.1 = (bf16[224,256]{1,0:T(8,128)(2,1)S(1)}, bf16[224,256]{1,0:T(8,128)(2,1)}, u32[]{:S(2)}) copy-start(bf16[224,256]{1,0:T(8,128)(2,1)} %get-tuple-element.7) | copy-start | bytes 344068
  187.5 0.9 copy-start

commit v5 on v4

--- a/solution.py
+++ b/solution.py
@@ -28,13 +28,13 @@
     ring,
     sections,
     x_ref,
-    froute_ref,
-    fweight_ref,
+    froute_hbm,
+    fweight_hbm,
     c_ref,
-    broute_ref,
-    bweight_ref,
-    sgate_ref,
-    sup_ref,
+    broute_hbm,
+    bweight_hbm,
+    sgate_hbm,
+    sup_hbm,
     wg_hbm,
     wu_hbm,
     wd_hbm,
@@ -42,9 +42,16 @@
     bout_ref,
     own_ref,
     peer_ref,
+    broute_ref,
+    sgate_ref,
+    sup_ref,
+    bweight_ref,
+    froute_ref,
+    fweight_ref,
     wg_ref,
     wu_ref,
     wd_ref,
+    result,
     gath_f,
     gath_b,
     red_f,
@@ -63,6 +70,7 @@
     dg,
     load_sem,
     keep_sem,
+    out_sem,
     pipe_send,
     pipe_recv,
     gs,
@@ -73,8 +81,8 @@
     dp_recv,
 ):
     width, rows = x_ref.shape
-    units = wg_ref.shape[0]
-    capacity = sgate_ref.shape[1]
+    units = wg_hbm.shape[0]
+    capacity = sgate_hbm.shape[1]
     half = ring // 2
     groups = ring // GROUP
     me = lax.axis_index("expert")
@@ -91,13 +99,6 @@
     sides = (right, left)
     stage = (ahead, behind)
 
-    loads = [
-        pltpu.make_async_copy(hbm, ref, load_sem.at[i])
-        for i, (hbm, ref) in enumerate(((wg_hbm, wg_ref), (wu_hbm, wu_ref), (wd_hbm, wd_ref)))
-    ]
-    for load in loads:
-        load.start()
-
     barrier = pltpu.get_barrier_semaphore()
     partners = [{"expert": right}, {"expert": left}, {"dp": peer}]
     for section_to in stage:
@@ -105,6 +106,24 @@
         partners += [{"pipe": section_to, "expert": side} for side in sides]
     for partner in partners:
         pl.semaphore_signal(barrier, inc=1, device_id=partner, device_id_type=MESH)
+    loads = [
+        pltpu.make_async_copy(hbm, ref, load_sem.at[i])
+        for i, (hbm, ref) in enumerate(
+            (
+                (broute_hbm, broute_ref),
+                (sgate_hbm, sgate_ref),
+                (sup_hbm, sup_ref),
+                (bweight_hbm, bweight_ref),
+                (froute_hbm, froute_ref),
+                (fweight_hbm, fweight_ref),
+                (wg_hbm, wg_ref),
+                (wu_hbm, wu_ref),
+                (wd_hbm, wd_ref),
+            )
+        )
+    ]
+    for load in loads:
+        load.start()
     pl.semaphore_wait(barrier, len(partners))
 
     def band(h):
@@ -135,6 +154,9 @@
             first(stream, h, way).start()
     for stream in range(2):
         shift(stream).start()
+
+    for load in loads:
+        load.wait()
 
     def split_weights(g):
         columns = pl.ds(pl.multiple_of(g * (GROUP * width), LANES), GROUP * width)
@@ -232,8 +254,6 @@
         use(k)
         return carry
 
-    for load in loads:
-        load.wait()
     lax.fori_loop(0, opening, gather_first, 0)
     shift(0).wait_recv()
     use_f(me)
@@ -337,6 +357,13 @@
     keep.start()
     lax.fori_loop(groups + 1, half, late, 0)
 
+    def deliver(stream, h):
+        return pltpu.make_async_copy(
+            result.at[stream, band(h)],
+            (fout_ref, bout_ref)[stream].at[band(h)],
+            out_sem.at[stream, h],
+        )
+
     for stream, h in flows:
         buf = (red_f, red_b)[stream]
         total = part(stream, h, me)
@@ -347,9 +374,11 @@
         summed = total.astype(BF16).astype(F32)
         if stream == 0:
             own = gath_f[me, band(h)].astype(F32)
-            fout_ref[band(h)] = (own + fweight_ref[...].astype(F32) * summed).astype(BF16)
+            out = own + fweight_ref[...].astype(F32) * summed
         else:
-            bout_ref[band(h)] = (gath_b[me, band(h)].astype(F32) + summed).astype(BF16)
+            out = gath_b[me, band(h)].astype(F32) + summed
+        result[stream, band(h)] = out.astype(BF16)
+        deliver(stream, h).start()
 
     shift(0).wait_send()
     shift(1).wait_send()
@@ -367,6 +396,8 @@
                 return carry
 
             lax.fori_loop(1, hops[h][way], drain, 0)
+    for stream, h in flows:
+        deliver(stream, h).wait()
 
 
 def solution(mesh):
@@ -390,8 +421,8 @@
         rows, width = fwd_sent.shape[1:]
         units, model = gate_weight.shape[1:]
         dma = pltpu.SemaphoreType.DMA
-        vmem = pl.BlockSpec(memory_space=pltpu.VMEM)
-        anywhere = pl.BlockSpec(memory_space=pl.ANY)
+        hbm = pl.BlockSpec(memory_space=pltpu.HBM)
+        capacity = saved_gate.shape[2]
         outs = pl.pallas_call(
             functools.partial(kernel, ring, sections),
             out_shape=(
@@ -400,12 +431,19 @@
                 jax.ShapeDtypeStruct((units // 2, model), F32),
                 jax.ShapeDtypeStruct((units // 2, model), F32),
             ),
-            in_specs=[vmem] * 8 + [anywhere] * 3,
-            out_specs=(vmem,) * 2 + (anywhere,) * 2,
+            in_specs=[hbm] * 11,
+            out_specs=(hbm,) * 4,
             scratch_shapes=[
+                pltpu.VMEM((1, rows), jnp.int32),
+                pltpu.VMEM((units, capacity), BF16),
+                pltpu.VMEM((units, capacity), BF16),
+                pltpu.VMEM((1, rows), BF16),
+                pltpu.VMEM((1, rows), jnp.int32),
+                pltpu.VMEM((1, rows), BF16),
                 pltpu.VMEM((units, model), BF16),
                 pltpu.VMEM((units, model), BF16),
                 pltpu.VMEM((units, model), BF16),
+                pltpu.VMEM((2, width, rows), BF16),
                 pltpu.VMEM((ring, width, rows), BF16),
                 pltpu.VMEM((ring, width, rows), BF16),
                 pltpu.VMEM((2, 2, half + 1, width // 2, rows), BF16),
@@ -422,8 +460,9 @@
                 pltpu.VMEM((units, rows), BF16),
                 pltpu.VMEM((2 * units, rows), BF16),
                 pltpu.VMEM((units, model), F32),
-                dma((3,)),
+                dma((9,)),
                 dma,
+                dma((2, 2)),
                 dma((2,)),
                 dma((2,)),
             ]

time: 190 us -> 188 us (0.989)
  no operation moved by 1% of the time
where the time goes in v5:
time: 188 us
  Pallas kernels  183 us (97%)
  other arithmetic  2.5 us (1%)
    pallas_call x1, Pallas kernels, body(): pl.pallas_call(functools.partial(kernel, ring, sections), out_shape=(jax....  183 us

profile of v5, /device:TPU:24, one launch (start us, length us, event | category | flops | bytes accessed | tf_op | source)
XLA Modules:
  0.0 187.8 jit_solution(2273519981246821253)
XLA Ops:
  0.6 183.1 %shard_map.130 = (bf16[224,256]{1,0:T(8,128)(2,1)}, bf16[224,256]{1,0:T(8,128)(2,1)}, f32[32,7168]{1,0:T(8,128)}, f32[32,7168]{1,0:T(8,128)}) custom-call(bf16[224,256]{1,0:T(8,128)(2,1)} %bitcast.32, s32[1,256]{1,0:T(1,128)} %bitcast.36, bf16[1,256]{1,0:T(2,128)(2,1)} %bitcast.37, bf16[224,256]{1,0:T(8,128)(2,1)} %bitcast.33, s32[1,256]{1,0:T(1,128)} %bitcast.38, ...), custom_call_target="tpu_custom_call" | custom-call | tf_op jit(solution)/shard_map/pallas_call | solution.py:426
  183.7 0.0 copy-start.1
  183.7 2.5 %add_bitcast_fusion = f32[1,32,7168]{2,1,0:T(8,128)} fusion(f32[32,7168]{1,0:T(8,128)} %get-tuple-element.9, f32[32,7168]{1,0:T(8,128)} %get-tuple-element.10), kind=kLoop, calls=%fused_computation | loop fusion | flops 229376 | bytes 2752512 | tf_op jit(solution)/shard_map/broadcast_in_dim | solution.py:487
  186.2 0.0 copy-done.1
  186.2 0.0 copy-start
  186.2 0.6 copy.16
  186.9 0.3 copy-done
  187.2 0.6 copy.17
Async XLA Ops:
  183.7 2.5 %copy-start.1 = (bf16[224,256]{1,0:T(8,128)(2,1)S(1)}, bf16[224,256]{1,0:T(8,128)(2,1)}, u32[]{:S(2)}) copy-start(bf16[224,256]{1,0:T(8,128)(2,1)} %get-tuple-element.7) | copy-start | bytes 344068
  186.2 0.9 copy-start

commit v6 on v5

--- a/solution.py
+++ b/solution.py
@@ -40,8 +40,7 @@
     wd_hbm,
     fout_ref,
     bout_ref,
-    own_ref,
-    peer_ref,
+    dgrad_ref,
     broute_ref,
     sgate_ref,
     sup_ref,
@@ -68,6 +67,7 @@
     hid,
     dgu,
     dg,
+    dg_in,
     load_sem,
     keep_sem,
     out_sem,
@@ -95,7 +95,7 @@
 
     part_width = width // 2
     hops = ((half, half - 1), (half - 1, half))
-    flows = [(stream, h) for h in range(2) for stream in range(2)]
+    flows = [(stream, h) for stream in range(2) for h in range(2)]
     sides = (right, left)
     stage = (ahead, behind)
 
@@ -342,7 +342,7 @@
     def give():
         return pltpu.make_async_remote_copy(
             src_ref=dg.at[pl.ds(pl.multiple_of(peer * (units // 2), 8), units // 2)],
-            dst_ref=peer_ref,
+            dst_ref=dg_in,
             send_sem=dp_send,
             recv_sem=dp_recv,
             device_id={"dp": peer},
@@ -350,12 +350,15 @@
         )
 
     mine_rows = pl.ds(pl.multiple_of(replica * (units // 2), 8), units // 2)
-    keep = pltpu.make_async_copy(dg.at[mine_rows], own_ref, keep_sem)
+    keep = pltpu.make_async_copy(dg_in, dgrad_ref, keep_sem)
 
     lax.fori_loop(1, groups + 1, early, 0)
     give().start()
+    lax.fori_loop(groups + 1, half, late, 0)
+
+    give().wait_recv()
+    dg_in[...] += dg[mine_rows, :]
     keep.start()
-    lax.fori_loop(groups + 1, half, late, 0)
 
     def deliver(stream, h):
         return pltpu.make_async_copy(
@@ -383,7 +386,6 @@
     shift(0).wait_send()
     shift(1).wait_send()
     give().wait_send()
-    give().wait_recv()
     keep.wait()
     for stream, h in flows:
         for way in range(2):
@@ -398,6 +400,23 @@
             lax.fori_loop(1, hops[h][way], drain, 0)
     for stream, h in flows:
         deliver(stream, h).wait()
+
+
+def hand_on(f_ref, b_ref, g_ref, fout_ref, bout_ref, gout_ref, sem, piece_sem):
+    copies = []
+    columns = g_ref.shape[1] // 2
+    for i in range(g_ref.shape[0] // 8):
+        for j in range(2):
+            piece = (pl.ds(8 * i, 8), pl.ds(columns * j, columns))
+            copies.append(
+                pltpu.make_async_copy(g_ref.at[piece], gout_ref.at[piece], piece_sem.at[i, j])
+            )
+    copies.append(pltpu.make_async_copy(f_ref, fout_ref, sem.at[0]))
+    copies.append(pltpu.make_async_copy(b_ref, bout_ref, sem.at[1]))
+    for copy in copies:
+        copy.start()
+    for copy in copies:
+        copy.wait()
 
 
 def solution(mesh):
@@ -429,10 +448,9 @@
                 jax.ShapeDtypeStruct((width, rows), BF16),
                 jax.ShapeDtypeStruct((width, rows), BF16),
                 jax.ShapeDtypeStruct((units // 2, model), F32),
-                jax.ShapeDtypeStruct((units // 2, model), F32),
             ),
             in_specs=[hbm] * 11,
-            out_specs=(hbm,) * 4,
+            out_specs=(hbm,) * 3,
             scratch_shapes=[
                 pltpu.VMEM((1, rows), jnp.int32),
                 pltpu.VMEM((units, capacity), BF16),
@@ -460,6 +478,7 @@
                 pltpu.VMEM((units, rows), BF16),
                 pltpu.VMEM((2 * units, rows), BF16),
                 pltpu.VMEM((units, model), F32),
+                pltpu.VMEM((units // 2, model), F32),
                 dma((9,)),
                 dma,
                 dma((2, 2)),
@@ -484,7 +503,14 @@
             up_weight[0],
             down_weight[0],
         )
-        return outs[0].T[None], outs[1].T[None], (outs[2] + outs[3])[None]
+        outs = pl.pallas_call(
+            hand_on,
+            out_shape=tuple(jax.ShapeDtypeStruct(out.shape, out.dtype) for out in outs),
+            in_specs=[hbm] * 3,
+            out_specs=(hbm,) * 3,
+            scratch_shapes=[dma((2,)), dma((units // 16, 2))],
+        )(*outs)
+        return outs[0].T[None], outs[1].T[None], outs[2][None]
 
     in_specs = (
         P("pipe", "dp", "expert"),

time: 188 us -> 220 us (1.17)
  Pallas kernels: 183 us -> 219 us
  other arithmetic: 2.5 us -> 0 us
    pallas_call x0 -> x1, Pallas kernels: none -> 35.9 us  [body(): pl.pallas_call(hand_on, out_shape=tuple((jax.ShapeDtypeStruct(out.shape,...]
    broadcast_in_dim x1 -> x0, other arithmetic: 2.5 us -> none  [body(): return (outs[0].T[None], outs[1].T[None], (outs[2] + outs[3])[None])]
where the time goes in v6:
time: 220 us; the launch traced here: 219 us
  Pallas kernels  219 us (100%)
    pallas_call x1, Pallas kernels, body(): pl.pallas_call(functools.partial(kernel, ring, sections), out_shape=(jax....  183 us
    pallas_call x1, Pallas kernels, body(): pl.pallas_call(hand_on, out_shape=tuple((jax.ShapeDtypeStruct(out.shape,...  35.9 us

profile of v6, /device:TPU:24, one launch (start us, length us, event | category | flops | bytes accessed | tf_op | source)
XLA Modules:
  0.0 219.2 jit_solution(17836815669133060645)
XLA Ops:
  0.6 182.6 %shard_map.130 = (bf16[224,256]{1,0:T(8,128)(2,1)}, bf16[224,256]{1,0:T(8,128)(2,1)}, f32[32,7168]{1,0:T(8,128)}) custom-call(bf16[224,256]{1,0:T(8,128)(2,1)} %bitcast.29, s32[1,256]{1,0:T(1,128)} %bitcast.33, bf16[1,256]{1,0:T(2,128)(2,1)} %bitcast.34, bf16[224,256]{1,0:T(8,128)(2,1)} %bitcast.30, s32[1,256]{1,0:T(1,128)} %bitcast.35, ...), custom_call_target="tpu_custom_call" | custom-call | tf_op jit(solution)/shard_map/pallas_call | solution.py:445
  183.2 35.9 %shard_map.131 = (bf16[224,256]{1,0:T(8,128)(2,1)}, bf16[224,256]{1,0:T(8,128)(2,1)}, f32[32,7168]{1,0:T(8,128)}) custom-call(bf16[224,256]{1,0:T(8,128)(2,1)} %get-tuple-element.9.f_ref, bf16[224,256]{1,0:T(8,128)(2,1)} %get-tuple-element.10.b_ref, f32[32,7168]{1,0:T(8,128)} %get-tuple-element.11.g_ref), custom_call_target="tpu_custom_call" | custom-call | tf_op jit(solution)/shard_map/pallas_call | solution.py:506

commit v7 on v6

--- a/solution.py
+++ b/solution.py
@@ -402,20 +402,23 @@
         deliver(stream, h).wait()
 
 
-def hand_on(f_ref, b_ref, g_ref, fout_ref, bout_ref, gout_ref, sem, piece_sem):
-    copies = []
+def hand_on(f_ref, b_ref, g_ref, fout_ref, bout_ref, gout_ref, f_held, b_held, g_held, sem, piece_sem):
+    pieces = []
     columns = g_ref.shape[1] // 2
     for i in range(g_ref.shape[0] // 8):
         for j in range(2):
             piece = (pl.ds(8 * i, 8), pl.ds(columns * j, columns))
-            copies.append(
-                pltpu.make_async_copy(g_ref.at[piece], gout_ref.at[piece], piece_sem.at[i, j])
-            )
-    copies.append(pltpu.make_async_copy(f_ref, fout_ref, sem.at[0]))
-    copies.append(pltpu.make_async_copy(b_ref, bout_ref, sem.at[1]))
-    for copy in copies:
+            pieces.append((g_ref.at[piece], g_held.at[piece], gout_ref.at[piece], piece_sem.at[i, j]))
+    pieces.append((f_ref, f_held, fout_ref, sem.at[0]))
+    pieces.append((b_ref, b_held, bout_ref, sem.at[1]))
+    come = [pltpu.make_async_copy(src, held, own.at[0]) for src, held, _, own in pieces]
+    go = [pltpu.make_async_copy(held, dst, own.at[1]) for _, held, dst, own in pieces]
+    for copy in come:
         copy.start()
-    for copy in copies:
+    for arrive, leave in zip(come, go):
+        arrive.wait()
+        leave.start()
+    for copy in go:
         copy.wait()
 
 
@@ -508,7 +511,8 @@
             out_shape=tuple(jax.ShapeDtypeStruct(out.shape, out.dtype) for out in outs),
             in_specs=[hbm] * 3,
             out_specs=(hbm,) * 3,
-            scratch_shapes=[dma((2,)), dma((units // 16, 2))],
+            scratch_shapes=[pltpu.VMEM(out.shape, out.dtype) for out in outs]
+            + [dma((2, 2)), dma((units // 16, 2, 2))],
         )(*outs)
         return outs[0].T[None], outs[1].T[None], outs[2][None]
 

time: 220 us -> 186 us (0.85)
  Pallas kernels: 219 us -> 185 us
    pallas_call x1, Pallas kernels: 35.9 us -> 2.18 us  [body(): pl.pallas_call(hand_on, out_shape=tuple((jax.ShapeDtypeStruct(out.shape,...]
where the time goes in v7:
time: 186 us; the launch traced here: 185 us
  Pallas kernels  185 us (99%)
    pallas_call x1, Pallas kernels, body(): pl.pallas_call(functools.partial(kernel, ring, sections), out_shape=(jax....  183 us

profile of v7, /device:TPU:24, one launch (start us, length us, event | category | flops | bytes accessed | tf_op | source)
XLA Modules:
  0.0 185.4 jit_solution(18058388317404523577)
XLA Ops:
  0.6 182.6 %shard_map.130 = (bf16[224,256]{1,0:T(8,128)(2,1)}, bf16[224,256]{1,0:T(8,128)(2,1)}, f32[32,7168]{1,0:T(8,128)}) custom-call(bf16[224,256]{1,0:T(8,128)(2,1)} %bitcast.29, s32[1,256]{1,0:T(1,128)} %bitcast.33, bf16[1,256]{1,0:T(2,128)(2,1)} %bitcast.34, bf16[224,256]{1,0:T(8,128)(2,1)} %bitcast.30, s32[1,256]{1,0:T(1,128)} %bitcast.35, ...), custom_call_target="tpu_custom_call" | custom-call | tf_op jit(solution)/shard_map/pallas_call | solution.py:448
  183.2 2.2 %shard_map.131 = (bf16[224,256]{1,0:T(8,128)(2,1)}, bf16[224,256]{1,0:T(8,128)(2,1)}, f32[32,7168]{1,0:T(8,128)}) custom-call(bf16[224,256]{1,0:T(8,128)(2,1)} %get-tuple-element.9.f_ref, bf16[224,256]{1,0:T(8,128)(2,1)} %get-tuple-element.10.b_ref, f32[32,7168]{1,0:T(8,128)} %get-tuple-element.11.g_ref), custom_call_target="tpu_custom_call" | custom-call | tf_op jit(solution)/shard_map/pallas_call | solution.py:509

commit v8 on v7

--- a/solution.py
+++ b/solution.py
@@ -318,6 +318,11 @@
         reduce(stream, h, way, k - 1).wait_recv()
         buf[h, way, k] = (buf[h, way, k].astype(F32) + term).astype(BF16)
         reduce(stream, h, way, k).start()
+        gather_copy(stream, h, way, k, me).wait_send()
+
+        @pl.when(k >= 2)
+        def _():
+            reduce(stream, h, way, k - 2).wait_send()
 
     def reduce_step(k):
         for stream, h in flows:
@@ -354,6 +359,11 @@
 
     lax.fori_loop(1, groups + 1, early, 0)
     give().start()
+    for stream in range(2):
+        shift(stream).wait_send()
+    for stream, h in flows:
+        for way in range(2):
+            first(stream, h, way).wait_send()
     lax.fori_loop(groups + 1, half, late, 0)
 
     give().wait_recv()
@@ -383,21 +393,12 @@
         result[stream, band(h)] = out.astype(BF16)
         deliver(stream, h).start()
 
-    shift(0).wait_send()
-    shift(1).wait_send()
     give().wait_send()
     keep.wait()
     for stream, h in flows:
         for way in range(2):
-            first(stream, h, way).wait_send()
-            reduce(stream, h, way, 0).wait_send()
-
-            def drain(k, carry):
-                gather_copy(stream, h, way, k, me).wait_send()
+            for k in range(max(hops[h][way] - 2, 0), hops[h][way]):
                 reduce(stream, h, way, k).wait_send()
-                return carry
-
-            lax.fori_loop(1, hops[h][way], drain, 0)
     for stream, h in flows:
         deliver(stream, h).wait()
 

time: 186 us -> 186 us (level)
  no operation moved by 1% of the time
where the time goes in v8:
time: 186 us; the launch traced here: 185 us
  Pallas kernels  184 us (99%)
    pallas_call x1, Pallas kernels, body(): pl.pallas_call(functools.partial(kernel, ring, sections), out_shape=(jax....  182 us

profile of v8, /device:TPU:24, one launch (start us, length us, event | category | flops | bytes accessed | tf_op | source)
XLA Modules:
  0.0 185.1 jit_solution(7198155811569336654)
XLA Ops:
  0.6 182.2 %shard_map.130 = (bf16[224,256]{1,0:T(8,128)(2,1)}, bf16[224,256]{1,0:T(8,128)(2,1)}, f32[32,7168]{1,0:T(8,128)}) custom-call(bf16[224,256]{1,0:T(8,128)(2,1)} %bitcast.29, s32[1,256]{1,0:T(1,128)} %bitcast.33, bf16[1,256]{1,0:T(2,128)(2,1)} %bitcast.34, bf16[224,256]{1,0:T(8,128)(2,1)} %bitcast.30, s32[1,256]{1,0:T(1,128)} %bitcast.35, ...), custom_call_target="tpu_custom_call" | custom-call | tf_op jit(solution)/shard_map/pallas_call | solution.py:449
  182.9 2.2 %shard_map.131 = (bf16[224,256]{1,0:T(8,128)(2,1)}, bf16[224,256]{1,0:T(8,128)(2,1)}, f32[32,7168]{1,0:T(8,128)}) custom-call(bf16[224,256]{1,0:T(8,128)(2,1)} %get-tuple-element.9.f_ref, bf16[224,256]{1,0:T(8,128)(2,1)} %get-tuple-element.10.b_ref, f32[32,7168]{1,0:T(8,128)} %get-tuple-element.11.g_ref), custom_call_target="tpu_custom_call" | custom-call | tf_op jit(solution)/shard_map/pallas_call | solution.py:510
